TPU v7x, 256 devices: a whole 4x4x8 slice. The times are simulated.
256 devices in a mesh: gx: 8 (over y, core), gy: 4 (over x), gz: 8 (over z).
Axes of the slice: x: 4, y: 4, z: 8, core: 2. Of those that a mesh axis runs over, the one named last changes fastest.
Arguments:
- tensor: float32 [4, 512, 512, 512], P(None, 'gx', 'gz', 'gy'), may hold values from -140 to 140, as said below
- starts: float32 [3, 512, 64], replicated, may hold values from -6 to 6
- trunc_ranks: int32 [3], replicated, may hold values from 32 to 64, as said below
Outputs:
- core_out: float32 [4, 64, 64, 64], P(None, ('gy', 'gz'), None, 'gx')
- factors: float32 [3, 512, 64], replicated
Inputs may be any that keep to these rules, and one draw needn't show every extreme that they name: `trunc_ranks`: each rank lies between 32 and 64; at least one mode has rank 64. `tensor`: entries are bounded in magnitude by 140.
All inputs are finite; a program needn't handle non-finite values.
Results may differ from a plain program's by a relative error of at most 0.0003.
Values sent between devices are 32-bit elements; how exact they have to be, the bound alone decides.
No kernel may reach another device: no remote copies, remote signals or barrier semaphores. Data moves between devices by JAX's collectives and lax.ppermute only.
A program may use at most 128 MiB of HBM per device.

v0:
```python
import jax
import jax.numpy as jnp
from jax import lax
from jax.sharding import PartitionSpec as P

ITERS = 4


def factor_from(local_gram, start_cols, rank_now):
    high = lax.Precision.HIGHEST
    gram_sum = lax.psum(local_gram, ("gx", "gy", "gz"))
    basis_now = start_cols
    for repeat in range(ITERS):
        image_cols = jnp.dot(gram_sum, basis_now, precision=high)
        inner_prod = jnp.dot(image_cols.T, image_cols, precision=high)
        lower_tri = jnp.linalg.cholesky(inner_prod)
        basis_now = lax.linalg.triangular_solve(
            lower_tri, image_cols, left_side=False, lower=True, transpose_a=True
        )
    keep_mask = (jnp.arange(start_cols.shape[1], dtype=jnp.int32) < rank_now).astype(jnp.float32)
    return basis_now * keep_mask[None, :]


def local(tensor, starts, trunc_ranks):
    high = lax.Precision.HIGHEST
    norm_scale = 1.0 / (tensor.shape[0] * starts.shape[1] * starts.shape[1])
    moved_one = lax.all_to_all(tensor, "gx", split_axis=3, concat_axis=1, tiled=True)
    gram_one = jnp.einsum("sipq,sjpq->ij", moved_one, moved_one, precision=high) * norm_scale
    first_u = factor_from(gram_one, starts[0], trunc_ranks[0])
    shrunk_one = jnp.einsum("sipq,ir->srpq", moved_one, first_u, precision=high)
    moved_two = lax.all_to_all(
        lax.all_to_all(shrunk_one, "gx", split_axis=2, concat_axis=3, tiled=True),
        "gy",
        split_axis=1,
        concat_axis=3,
        tiled=True,
    )
    gram_two = jnp.einsum("spqi,spqj->ij", moved_two, moved_two, precision=high) * norm_scale
    second_u = factor_from(gram_two, starts[1], trunc_ranks[1])
    shrunk_two = jnp.einsum("spqi,ir->spqr", moved_two, second_u, precision=high)
    moved_three = lax.all_to_all(
        lax.all_to_all(shrunk_two, "gx", split_axis=3, concat_axis=2, tiled=True),
        "gz",
        split_axis=1,
        concat_axis=2,
        tiled=True,
    )
    gram_three = jnp.einsum("spiq,spjq->ij", moved_three, moved_three, precision=high) * norm_scale
    third_u = factor_from(gram_three, starts[2], trunc_ranks[2])
    core_out = jnp.einsum("spiq,ir->sprq", moved_three, third_u, precision=high)
    return (core_out, jnp.stack([first_u, second_u, third_u]))


def solution(mesh):
    return jax.shard_map(
        local,
        mesh=mesh,
        in_specs=(P(None, "gx", "gz", "gy"), P(), P()),
        out_specs=(P(None, ("gy", "gz"), None, "gx"), P()),
        check_vma=False,
    )
```

profile of v0, /device:TPU:1, one launch (start us, length us, event | category | flops | bytes accessed | tf_op | source)
XLA Modules:
  0.0 1284.0 jit_solution(4929801876800500415)
XLA Ops:
  7.2 16.2 %copy.76 = f32[4,64,64,128]{2,1,0,3:T(8,128)} copy(f32[4,64,64,128]{3,2,1,0:T(8,128)} %param.6) | data formatting | bytes 16777216 | tf_op args[0]
  23.5 15.4 %reshape.82 = f32[8,1,262144]{2,1,0:T(1,128)} reshape(f32[128,4,64,64]{3,2,1,0:T(8,128)} %bitcast.288) | data formatting | bytes 16777216
  38.9 104.0 %all_to_all.90 = f32[8,1,262144]{2,1,0:T(1,128)} all-to-all(f32[8,1,262144]{2,1,0:T(1,128)} %reshape.82), channel_id=1, replica_groups=mesh['gx'=8,'gy'=4,'gz'=8] {'gx'}, dimensions={0} | all-to-all | bytes 16777216 | tf_op jit(solution)/shard_map/all_to_all | solution.py:27
  143.4 26.2 %reduce.4 = f32[8,262144]{1,0:T(8,128)} reduce(f32[8,1,262144]{2,1,0:T(1,128)} %all_to_all.90, f32[]{:T(128)} %broadcast.74), dimensions={1}, to_apply=%all_to_all.65.reduce_sub_computation | reduce | bytes 16777220 | tf_op jit(solution)/shard_map/all_to_all | solution.py:27
  169.6 15.6 %reshape.83 = f32[128,4,64,64]{3,2,1,0:T(8,128)} reshape(f32[8,262144]{1,0:T(8,128)} %reduce.4) | data formatting | bytes 16777216
  185.2 17.6 %copy.78 = f32[4,8,64,64,16]{2,1,3,0,4:T(8,128)} copy(f32[4,8,64,64,16]{3,2,0,4,1:T(8,128)} %bitcast.289) | data formatting | bytes 16777216 | tf_op jit(solution)/shard_map/all_to_all | solution.py:27
  202.9 14.2 %all_to_all.68 = f32[4,512,64,16]{1,2,0,3:T(8,128)} reshape(f32[4,8,64,64,16]{2,1,3,0,4:T(8,128)} %copy.78) | data formatting | bytes 16777216 | tf_op jit(solution)/shard_map/all_to_all | solution.py:27
  217.1 17.7 %fusion.6 = f32[512,512]{1,0:T(8,128)} fusion(f32[4,512,64,16]{1,2,0,3:T(8,128)} %all_to_all.68), kind=kOutput, calls=%fused_computation.7 | convolution fusion | flops 12885164032 | bytes 9437184 | tf_op jit(solution)/shard_map/sipq,sjpq->ij/dot_general | solution.py:28
  236.2 252.8 %all-reduce.4.cloned.1.call-done = f32[512,512]{1,0:T(8,128)} async-done(((f32[512,512]{1,0:T(8,128)}), f32[512,512]{1,0:T(8,128)}) %all-reduce.4.cloned.1.call-update) | async-done | bytes 1048592 | tf_op jit(solution)/shard_map/psum | solution.py:11
  491.7 5.8 cholesky.194
  506.8 5.8 cholesky.205
  522.0 5.8 cholesky.216
  537.1 5.8 cholesky.227
  549.6 15.7 %fusion.2 = f32[4,64,64,16]{2,1,3,0:T(8,128)} fusion(f32[4,512,64,16]{1,2,0,3:T(8,128)} %all_to_all.68, f32[512,64]{0,1:T(8,128)S(1)} %fusion.10), kind=kOutput, calls=%fused_computation.2 | convolution fusion | flops 1610612736 | bytes 9568256 | tf_op jit(solution)/shard_map/sipq,ir->srpq/dot_general | solution.py:30
  569.7 21.2 %all_to_all.91 = f32[8,1,32768]{2,1,0:T(1,128)S(1)} all-to-all(f32[8,1,32768]{2,1,0:T(1,128)S(1)} %reshape.84), channel_id=1, replica_groups=mesh['gx'=8,'gy'=4,'gz'=8] {'gx'}, dimensions={0} | all-to-all | bytes 2097152 | tf_op jit(solution)/shard_map/all_to_all | solution.py:32
  599.1 16.8 %all_to_all.92 = f32[4,64,8,128]{3,2,0,1:T(8,128)S(1)} all-to-all(f32[4,64,8,128]{3,2,0,1:T(8,128)S(1)} %copy.87), channel_id=1, replica_groups=mesh['gx'=8,'gy'=4,'gz'=8] {'gy'}, dimensions={1} | all-to-all | bytes 2097152 | tf_op jit(solution)/shard_map/all_to_all | solution.py:31
  621.0 251.1 %all-reduce.6.cloned.1.call-done = f32[512,512]{1,0:T(8,128)} async-done(((f32[512,512]{1,0:T(8,128)}), f32[512,512]{1,0:T(8,128)}) %all-reduce.6.cloned.1.call-update) | async-done | bytes 1048592 | tf_op jit(solution)/shard_map/psum | solution.py:11
  874.8 5.8 cholesky.238
  889.9 5.8 cholesky.249
  905.1 5.8 cholesky.260
  920.2 5.8 cholesky.271
  935.2 11.4 all_to_all.93
  949.2 12.7 all_to_all.94
  966.0 249.0 %all-reduce.8.cloned.1.call-done = f32[512,512]{1,0:T(8,128)} async-done(((f32[512,512]{1,0:T(8,128)}), f32[512,512]{1,0:T(8,128)}) %all-reduce.8.cloned.1.call-update) | async-done | bytes 1048592 | tf_op jit(solution)/shard_map/psum | solution.py:11
  (151 shorter events, 164.8 us)
Async XLA Ops:
  7.2 481.8 %all-reduce.4.cloned.1.call-start = ((), (), s32[]{:S(2)}) async-start(), calls=%async_computation.5 | async-start | bytes 2097152 | tf_op jit(solution)/shard_map/psum | solution.py:11
  217.1 17.8 %copy-start.1 = (s32[3]{0:T(128)S(1)}, s32[3]{0:T(128)}, u32[]{:S(2)}) copy-start(s32[3]{0:T(128)} %param.8) | copy-start | bytes 40
  234.8 637.3 %all-reduce.6.cloned.1.call-start = ((), (), s32[]{:S(2)}) async-start(), calls=%async_computation.6 | async-start | bytes 2097152 | tf_op jit(solution)/shard_map/psum | solution.py:11
  617.1 255.0 %copy-start = (f32[3,512,64]{1,2,0:T(8,128)S(1)}, f32[3,512,64]{1,2,0:T(8,128)}, u32[]{:S(2)}) copy-start(f32[3,512,64]{1,2,0:T(8,128)} %param.7) | copy-start | bytes 1179652
  620.0 595.0 %all-reduce.8.cloned.1.call-start = ((), (), s32[]{:S(2)}) async-start(), calls=%async_computation.7 | async-start | bytes 2097152 | tf_op jit(solution)/shard_map/psum | solution.py:11
Sparse Core Ops, SparseCore 0:
  234.9 254.0 all-reduce.3
  620.1 251.9 all-reduce.5
  965.5 249.4 all-reduce.7
where the time goes:
time: 1290 us; the launch traced here: 1280 us
  waiting for transfers between devices  753 us (58%)
  other arithmetic  179 us (14%)
  blocking collectives  166 us (13%)
  local copies, waits for them, and re-layouts  95 us (7%)
  matrix products  75.8 us (6%)
  between operations  14.6 us (1%)
    psum x3, waiting for transfers between devices, factor_from(): gram_sum = lax.psum(local_gram, ('gx', 'gy', 'gz'))  753 us
    all_to_all x1, blocking collectives, local(): lax.all_to_all(tensor, 'gx', split_axis=3, concat_axis=1, tiled=True)  104 us
    another operation x36, other arithmetic, factor_from(): lower_tri = jnp.linalg.cholesky(inner_prod)  78.2 us
    another operation x24, other arithmetic, factor_from(): lax.linalg.triangular_solve(lower_tri, image_cols, left_side=False, lower...  66.6 us
    unnamed x13, local copies, waits for them, and re-layouts  50.5 us
    all_to_all x3, local copies, waits for them, and re-layouts, local(): lax.all_to_all(tensor, 'gx', split_axis=3, concat_axis=1, tiled=True)  32.4 us
    dot_general x12, matrix products, factor_from(): image_cols = jnp.dot(gram_sum, basis_now, precision=high)  28.3 us
    all_to_all x1, other arithmetic, local(): lax.all_to_all(tensor, 'gx', split_axis=3, concat_axis=1, tiled=True)  26.2 us
  transfers between devices with their start and end apart: 3, of which 3 were waited for; matrix products, arithmetic and copies ran while one was open for 0% of the time, Pallas kernels for 0%

commit v1 on v0

v1 whole, which is shorter than its diff:
```python
import jax
import jax.numpy as jnp
from jax import lax
from jax.experimental import pallas as pl
from jax.experimental.pallas import tpu as pltpu
from jax.sharding import PartitionSpec as P

N = 512
R = 64
ITERS = 4
BF = jnp.bfloat16
F32 = jnp.float32
PAIRS = [(a, b) for a in range(4) for b in range(a, 4)]
NT = (((1,), (1,)), ((), ()))
NN = (((1,), (0,)), ((), ()))
VMEM = pl.BlockSpec(memory_space=pltpu.VMEM)
SMEM = pl.BlockSpec(memory_space=pltpu.SMEM)
ANY = pl.BlockSpec(memory_space=pl.ANY)


def split(x):
    hi = x.astype(BF)
    return hi, (x - hi.astype(F32)).astype(BF)


def mm(a, b, dims=NN):
    return lax.dot_general(a, b, dims, preferred_element_type=F32)


def put_blocks(out_ref, low, high):
    for n, (a, b) in enumerate(PAIRS):
        if a < 2:
            out_ref[n] = low[a * 128 : a * 128 + 128, b * 128 : b * 128 + 128]
        else:
            out_ref[n] = high[a * 128 - 256 : a * 128 - 128, b * 128 - 256 : b * 128 - 128]


def inverse_factor(cc):
    row8 = lax.broadcasted_iota(jnp.int32, (8, 128), 0)
    lane = lax.broadcasted_iota(jnp.int32, (8, 128), 1)
    m = [
        jnp.where(lane < R, (lane == row8 + 8 * b).astype(F32), cc[8 * b : 8 * b + 8, :])
        for b in range(8)
    ]
    scale = [jnp.ones((8, 128), F32) for _ in range(8)]
    for j0 in range(0, R, 4):
        b0 = j0 // 8
        cols = [
            [jnp.broadcast_to(m[b][:, R + j0 + k : R + j0 + k + 1], (8, 128)) for b in range(b0, 8)]
            for k in range(4)
        ]
        for k in range(4):
            r = (j0 + k) % 8
            pivot = cols[k][0][r : r + 1, :]
            inv = 1.0 / pivot
            scaled_row = m[b0][r : r + 1, :] * inv
            factors = [cols[k2][0][r : r + 1, :] * inv for k2 in range(k + 1, 4)]
            scale[b0] = jnp.where(row8 == r, pivot, scale[b0])
            for b in range(b0, 8):
                c = cols[k][b - b0]
                if b == b0:
                    c = jnp.where(row8 > r, c, 0.0)
                m[b] = m[b] - c * scaled_row
                for k2 in range(k + 1, 4):
                    cols[k2][b - b0] = cols[k2][b - b0] - c * factors[k2 - k - 1]
    out = []
    for b in range(8):
        y = lax.rsqrt(scale[b])
        y = y * (1.5 - 0.5 * (scale[b] * y) * y)
        out.append(m[b] * y)
    return jnp.concatenate(out, axis=0)


def subspace(gt_ref, start, gh_ref, gl_ref):
    for n, (a, b) in enumerate(PAIRS):
        blk = gt_ref[n]
        hi, lo = split(blk)
        gh_ref[a * 128 : a * 128 + 128, b * 128 : b * 128 + 128] = hi
        gl_ref[a * 128 : a * 128 + 128, b * 128 : b * 128 + 128] = lo
        if a != b:
            hi, lo = split(blk.T)
            gh_ref[b * 128 : b * 128 + 128, a * 128 : a * 128 + 128] = hi
            gl_ref[b * 128 : b * 128 + 128, a * 128 : a * 128 + 128] = lo

    lane = lax.broadcasted_iota(jnp.int32, (R, 128), 1)

    def step(_, v):
        vh, vl = split(v)
        t = mm(jnp.concatenate([vh, vl], axis=0), gh_ref[...])
        w = t[:R] + t[R:] + mm(vh, gl_ref[...])
        wh, wl = split(w)
        ws = jnp.concatenate([wh, wl], axis=0)
        c = mm(ws, ws, NT)
        c = c[:R] + c[R:]
        li = inverse_factor(c + pltpu.roll(c, R, 1))
        lh = li.astype(BF).astype(F32)
        both = jnp.where(lane < R, lh, pltpu.roll(li - lh, R, 1)).astype(BF)
        return mm(
            jnp.concatenate([both, both], axis=1),
            jnp.concatenate([wh, wh, wl, wl], axis=0),
        )

    return lax.fori_loop(0, ITERS, step, start)


def masked_factor(gt_ref, start_ref, rank_ref, mode, gh_ref, gl_ref, u_ref):
    v = subspace(gt_ref, start_ref[mode], gh_ref, gl_ref)
    row = lax.broadcasted_iota(jnp.int32, (R, N), 0)
    v = jnp.where(row < rank_ref[mode], v, 0.0)
    u_ref[...] = jnp.concatenate([v, v], axis=0).T[:, :R]
    return v


def gram_one_kernel(x_ref, g_ref, xh_ref, xl_ref, low_ref, high_ref):
    step = pl.program_id(0)

    @pl.when(step == 0)
    def _():
        low_ref[...] = jnp.zeros_like(low_ref)
        high_ref[...] = jnp.zeros_like(high_ref)

    for p in range(8):
        for g in range(8):
            hi, lo = split(x_ref[g, 0, pl.ds(p, 64, stride=8), :])
            xh_ref[p, g * 64 : g * 64 + 64, :] = hi
            xl_ref[p, g * 64 : g * 64 + 64, :] = lo
    for p in range(0, 8, 4):
        xh = jnp.concatenate([xh_ref[p + k] for k in range(4)], axis=1)
        xl = jnp.concatenate([xl_ref[p + k] for k in range(4)], axis=1)
        low_ref[...] += mm(xh[:256], xh, NT) + mm(xh[:256], xl, NT) + mm(xl[:256], xh, NT)
        high_ref[...] += (
            mm(xh[256:], xh[256:], NT) + mm(xh[256:], xl[256:], NT) + mm(xl[256:], xh[256:], NT)
        )

    @pl.when(step == pl.num_programs(0) - 1)
    def _():
        put_blocks(g_ref, low_ref[...] * 2.0**-20, high_ref[...] * 2.0**-20)


def gram_one(x):
    return pl.pallas_call(
        gram_one_kernel,
        grid=(4,),
        out_shape=(
            jax.ShapeDtypeStruct((10, 128, 128), F32),
            jax.ShapeDtypeStruct((8, N, N), BF),
            jax.ShapeDtypeStruct((8, N, N), BF),
        ),
        in_specs=[pl.BlockSpec((8, 1, N, 128), lambda i: (0, i, 0, 0))],
        out_specs=(
            pl.BlockSpec((10, 128, 128), lambda i: (0, 0, 0)),
            pl.BlockSpec((8, N, 128), lambda i: (0, 0, i)),
            pl.BlockSpec((8, N, 128), lambda i: (0, 0, i)),
        ),
        scratch_shapes=[pltpu.VMEM((256, N), F32), pltpu.VMEM((256, 256), F32)],
        compiler_params=pltpu.CompilerParams(vmem_limit_bytes=40 * 2**20),
        name="gram_one",
    )(x)


def factor_one_kernel(
    gt_ref, start_ref, rank_ref, xh_hbm, xl_hbm, u_ref, a_ref, g_ref, gh_ref, gl_ref, xh_ref, xl_ref, sem
):
    copies = [
        pltpu.make_async_copy(xh_hbm, xh_ref, sem.at[0]),
        pltpu.make_async_copy(xl_hbm, xl_ref, sem.at[1]),
    ]
    for c in copies:
        c.start()
    v = masked_factor(gt_ref, start_ref, rank_ref, 0, gh_ref, gl_ref, u_ref)
    vh, vl = split(v)
    vs = jnp.concatenate([vh, vl], axis=0)
    for c in copies:
        c.wait()
    for p in range(8):
        t = mm(vs, xh_ref[p])
        y = t[:R] + t[R:] + mm(vh, xl_ref[p])
        for q in range(4):
            a_ref[q, pl.ds(p, R, stride=8), :] = y[:, 128 * q : 128 * q + 128]
    a = jnp.concatenate([a_ref[q] for q in range(4)], axis=1)
    ah, al = split(a)
    th, tl = split(a.T)
    low = mm(th[:256], ah) + mm(th[:256], al) + mm(tl[:256], ah)
    high = mm(th[256:], ah[:, 256:]) + mm(th[256:], al[:, 256:]) + mm(tl[256:], ah[:, 256:])
    put_blocks(g_ref, low * 2.0**-20, high * 2.0**-20)


def factor_one(gt, starts, ranks, xh, xl):
    return pl.pallas_call(
        factor_one_kernel,
        out_shape=(
            jax.ShapeDtypeStruct((N, R), F32),
            jax.ShapeDtypeStruct((4, N, 128), F32),
            jax.ShapeDtypeStruct((10, 128, 128), F32),
        ),
        in_specs=[VMEM, VMEM, SMEM, ANY, ANY],
        out_specs=(VMEM, VMEM, VMEM),
        scratch_shapes=[
            pltpu.VMEM((N, N), BF),
            pltpu.VMEM((N, N), BF),
            pltpu.VMEM((8, N, N), BF),
            pltpu.VMEM((8, N, N), BF),
            pltpu.SemaphoreType.DMA((2,)),
        ],
        compiler_params=pltpu.CompilerParams(vmem_limit_bytes=40 * 2**20),
        name="factor_one",
    )(gt, starts, ranks, xh, xl)


def factor_two_kernel(gt_ref, start_ref, rank_ref, a_ref, u_ref, y_ref, gh_ref, gl_ref):
    v = masked_factor(gt_ref, start_ref, rank_ref, 1, gh_ref, gl_ref, u_ref)
    vh, vl = split(v)
    vs = jnp.concatenate([vh, vl], axis=0)
    ah, al = split(jnp.concatenate([a_ref[q] for q in range(4)], axis=1))
    y = mm(ah, vs, NT) + mm(al, vs, NT)
    y = y + pltpu.roll(y, R, 1)
    rolled = [y if k == 0 else pltpu.roll(y, 8 * k, 1) for k in range(8)]
    group = lax.broadcasted_iota(jnp.int32, (8, 128), 1) // 8
    for bx in range(8):
        for by in range(4):
            tile = jnp.zeros((8, 128), F32)
            for r in range(16):
                at = (by * 16 + r) * 8
                tile = jnp.where(group == r, rolled[(r - bx) % 8][at : at + 8, :], tile)
            y_ref[bx * 4 + by] = tile


def factor_two(gt, starts, ranks, a):
    return pl.pallas_call(
        factor_two_kernel,
        out_shape=(
            jax.ShapeDtypeStruct((N, R), F32),
            jax.ShapeDtypeStruct((32, 8, 128), F32),
        ),
        in_specs=[VMEM, VMEM, SMEM, VMEM],
        out_specs=(VMEM, VMEM),
        scratch_shapes=[pltpu.VMEM((N, N), BF), pltpu.VMEM((N, N), BF)],
        compiler_params=pltpu.CompilerParams(vmem_limit_bytes=32 * 2**20),
        name="factor_two",
    )(gt, starts, ranks, a)


def columns(b_ref):
    return jnp.concatenate(
        [b_ref[:, 8 * s : 8 * s + 8].reshape(N, 128) for s in range(4)], axis=1
    )


def gram_three_kernel(b_ref, g_ref):
    bh, bl = split(columns(b_ref))
    low = mm(bh[:256], bh, NT) + mm(bh[:256], bl, NT) + mm(bl[:256], bh, NT)
    high = mm(bh[256:], bh[256:], NT) + mm(bh[256:], bl[256:], NT) + mm(bl[256:], bh[256:], NT)
    put_blocks(g_ref, low * 2.0**-20, high * 2.0**-20)


def gram_three(b):
    return pl.pallas_call(
        gram_three_kernel,
        out_shape=jax.ShapeDtypeStruct((10, 128, 128), F32),
        in_specs=[VMEM],
        out_specs=VMEM,
        compiler_params=pltpu.CompilerParams(vmem_limit_bytes=32 * 2**20),
        name="gram_three",
    )(b)


def factor_three_kernel(gt_ref, start_ref, rank_ref, place_ref, b_ref, u_ref, core_ref, gh_ref, gl_ref):
    v = masked_factor(gt_ref, start_ref, rank_ref, 2, gh_ref, gl_ref, u_ref)
    vh, vl = split(v)
    bh, bl = split(columns(b_ref))
    t = mm(jnp.concatenate([vh, vl], axis=0), bh)
    core = t[:R] + t[R:] + mm(vh, bl)
    shift = (8 - place_ref[0]) * 16
    for s in range(4):
        part = pltpu.roll(core[:, s * 128 : s * 128 + 128], shift, 1)
        core_ref[s, 0] = part[:, 0:8]
        core_ref[s, 1] = part[:, 8:16]


def factor_three(gt, starts, ranks, place, b):
    return pl.pallas_call(
        factor_three_kernel,
        out_shape=(
            jax.ShapeDtypeStruct((N, R), F32),
            jax.ShapeDtypeStruct((4, 2, R, 8), F32),
        ),
        in_specs=[VMEM, VMEM, SMEM, SMEM, VMEM],
        out_specs=(VMEM, VMEM),
        scratch_shapes=[pltpu.VMEM((N, N), BF), pltpu.VMEM((N, N), BF)],
        compiler_params=pltpu.CompilerParams(vmem_limit_bytes=32 * 2**20),
        name="factor_three",
    )(gt, starts, ranks, place, b)


PLANE = ("gx", "gy")


def swap(x, axes):
    return lax.all_to_all(x, axes, 0, 0, tiled=True)


def spread(x, axes, count):
    return swap(jnp.broadcast_to(x[None], (count,) + x.shape), axes)


def sum_plane(g):
    return jnp.sum(swap(g.reshape(32, 40, 128), PLANE), axis=0)


def local(tensor, starts, trunc_ranks):
    starts_t = jnp.swapaxes(starts, 1, 2)
    place = lax.axis_index("gz").astype(jnp.int32).reshape(1)
    x = tensor.reshape(4, 64, 8, 8, 128).transpose(0, 2, 1, 3, 4).reshape(32, N, 128)
    x = swap(x, PLANE).reshape(8, 4, N, 128)
    g, xh, xl = gram_one(x)
    g = jnp.sum(spread(sum_plane(g), "gz", 8), axis=0)
    g = spread(g, PLANE, 32).reshape(10, 128, 128)
    u_one, a, g = factor_one(g, starts_t, trunc_ranks, xh, xl)
    g = jnp.sum(spread(sum_plane(g), "gz", 8), axis=0)
    g = spread(g, PLANE, 32).reshape(10, 128, 128)
    u_two, y = factor_two(g, starts_t, trunc_ranks, a)
    b = spread(swap(y, PLANE), "gz", 8)
    g = sum_plane(gram_three(b))
    g = spread(g, PLANE, 32).reshape(10, 128, 128)
    u_three, core_out = factor_three(g, starts_t, trunc_ranks, place, b)
    return (core_out, jnp.stack([u_one, u_two, u_three]))


def solution(mesh):
    return jax.shard_map(
        local,
        mesh=mesh,
        in_specs=(P(None, "gx", "gz", "gy"), P(), P()),
        out_specs=(P(None, ("gy", "gz"), None, "gx"), P()),
        check_vma=False,
    )
```

time: 1290 us -> 347 us (0.27)
  waiting for transfers between devices: 753 us -> 12.5 us
  other arithmetic: 179 us -> 0.24 us
  blocking collectives: 166 us -> 261 us
  local copies, waits for them, and re-layouts: 95 us -> 15.5 us
  matrix products: 75.8 us -> 0 us
  Pallas kernels: 0 us -> 51.7 us
  between operations: 14.6 us -> 0.75 us
    psum x3 -> x0, waiting for transfers between devices: 753 us -> none  [factor_from(): gram_sum = lax.psum(local_gram, ('gx', 'gy', 'gz'))]
    another operation x61 -> x1, other arithmetic: 146 us -> 0.06 us  [local(): return (core_out, jnp.stack([u_one, u_two, u_three]))]
    all_to_all x5 -> x10, blocking collectives: 166 us -> 261 us  [swap(): return lax.all_to_all(x, axes, 0, 0, tiled=True)]
    dot_general x30 -> x0, matrix products: 71.8 us -> none  [the longest x12 28.3 us: factor_from(): image_cols = jnp.dot(gram_sum, basis_now, precision=high)]
    pallas_call x0 -> x5, Pallas kernels: none -> 51.7 us  [the longest x1 15.4 us: factor_one(): pl.pallas_call(factor_one_kernel, out_shape=(jax.ShapeDtypeStruct((N, R),...]
    unnamed x13 -> x14, local copies, waits for them, and re-layouts: 50.5 us -> 10 us
    all_to_all x11 -> x0, local copies, waits for them, and re-layouts: 38.9 us -> none  [the longest x3 32.4 us: local(): lax.all_to_all(tensor, 'gx', split_axis=3, concat_axis=1, tiled=True)]
    all_to_all x4 -> x0, other arithmetic: 31.3 us -> none  [the longest x1 26.2 us: local(): lax.all_to_all(tensor, 'gx', split_axis=3, concat_axis=1, tiled=True)]
  transfers between devices with their start and end apart: 3 -> 1, of which waited for: 3 -> 1; matrix products, arithmetic and copies ran while one was open for 0% -> 0% of each run, Pallas kernels for 0% -> 0%
where the time goes in v1:
time: 347 us; the launch traced here: 346 us
  blocking collectives  261 us (75%)
  Pallas kernels  51.7 us (15%)
  local copies, waits for them, and re-layouts  15.5 us (4%)
  waiting for transfers between devices  12.5 us (4%)
  starting transfers between devices  4.57 us (1%)
    all_to_all x10, blocking collectives, swap(): return lax.all_to_all(x, axes, 0, 0, tiled=True)  261 us
    pallas_call x1, Pallas kernels, factor_one(): pl.pallas_call(factor_one_kernel, out_shape=(jax.ShapeDtypeStruct((N, R),...  15.4 us
    pallas_call x1, Pallas kernels, factor_two(): pl.pallas_call(factor_two_kernel, out_shape=(jax.ShapeDtypeStruct((N, R),...  13.1 us
    pallas_call x1, Pallas kernels, factor_three(): pl.pallas_call(factor_three_kernel, out_shape=(jax.ShapeDtypeStruct((N, R...  12.7 us
    all_to_all x1, waiting for transfers between devices, swap(): return lax.all_to_all(x, axes, 0, 0, tiled=True)  12.5 us
    unnamed x14, local copies, waits for them, and re-layouts  10 us
    pallas_call x1, Pallas kernels, gram_one(): pl.pallas_call(gram_one_kernel, grid=(4,), out_shape=(jax.ShapeDtypeStruc...  9.76 us
  transfers between devices with their start and end apart: 1, of which 1 were waited for; matrix products, arithmetic and copies ran while one was open for 0% of the time, Pallas kernels for 0%

profile of v1, /device:TPU:1, one launch (start us, length us, event | category | flops | bytes accessed | tf_op | source)
XLA Modules:
  0.0 346.0 jit_solution(317701849292265879)
XLA Ops:
  0.6 4.4 %copy.8 = f32[4,8,64,8,128]{4,3,2,1,0:T(8,128)S(1)} copy(f32[4,8,64,8,128]{4,3,1,2,0:T(8,128)} %bitcast.30) | data formatting | bytes 16777216 | tf_op jit(solution)/shard_map/transpose | solution.py:313
  5.1 103.2 %all_to_all.55 = f32[32,512,128]{2,1,0:T(8,128)} all-to-all(f32[32,512,128]{2,1,0:T(8,128)S(1)} %bitcast.29), channel_id=1, replica_groups=mesh['gx'=8,'gy'=4,'gz'=8] {'gx','gy'}, dimensions={0} | all-to-all | bytes 16777216 | tf_op jit(solution)/shard_map/all_to_all | solution.py:299
  108.2 9.8 %gram_one.1 = (f32[10,128,128]{2,1,0:T(8,128)S(1)}, bf16[8,512,512]{2,1,0:T(8,128)(2,1)S(1)}, bf16[8,512,512]{2,1,0:T(8,128)(2,1)S(1)}) custom-call(f32[8,4,512,128]{3,2,1,0:T(8,128)} %bitcast.28), custom_call_target="tpu_custom_call" | custom-call | tf_op jit(solution)/shard_map/gram_one/pallas_call | solution.py:141
  118.0 1.9 copy-done
  119.9 2.0 copy-done.2
  121.9 17.6 %all_to_all.56 = f32[32,40,128]{2,1,0:T(8,128)S(1)} all-to-all(f32[32,40,128]{2,1,0:T(8,128)S(1)} %bitcast.24), channel_id=1, replica_groups=mesh['gx'=8,'gy'=4,'gz'=8] {'gx','gy'}, dimensions={0} | all-to-all | bytes 1310720 | tf_op jit(solution)/shard_map/all_to_all | solution.py:299
  139.6 16.1 %all_to_all.57 = f32[8,40,128]{2,1,0:T(8,128)S(1)} all-to-all(f32[8,40,128]{2,1,0:T(8,128)S(1)} %broadcast_in_dim.12), channel_id=1, replica_groups=mesh['gx'=8,'gy'=4,'gz'=8] {'gz'}, dimensions={0} | all-to-all | bytes 327680 | tf_op jit(solution)/shard_map/all_to_all | solution.py:299
  155.7 18.5 %all_to_all.58 = f32[32,40,128]{2,1,0:T(8,128)S(1)} all-to-all(f32[32,40,128]{2,1,0:T(8,128)S(1)} %broadcast_in_dim.13), channel_id=1, replica_groups=mesh['gx'=8,'gy'=4,'gz'=8] {'gx','gy'}, dimensions={0} | all-to-all | bytes 1310720 | tf_op jit(solution)/shard_map/all_to_all | solution.py:299
  174.2 2.2 copy-done.1
  176.4 2.2 copy-done.3
  178.6 15.4 %factor_one.1 = (f32[512,64]{1,0:T(8,128)S(1)}, f32[4,512,128]{2,1,0:T(8,128)S(1)}, f32[10,128,128]{2,1,0:T(8,128)S(1)}) custom-call(f32[10,128,128]{2,1,0:T(8,128)S(1)} %bitcast.19, f32[3,64,512]{2,1,0:T(8,128)S(1)} %bitcast.16, s32[3]{0:T(128)S(1)} %copy-done.5, bf16[8,512,512]{2,1,0:T(8,128)(2,1)S(1)} %copy-done.1, bf16[8,512,512]{2,1,0:T(8,128)(2,1)S(1)} %copy-done.3), custom_call_target="tpu_custom_call" | custom-call | tf_op jit(solution)/shard_map/factor_one/pallas_call | solution.py:189
  194.0 16.9 %all_to_all.59 = f32[32,40,128]{2,1,0:T(8,128)S(1)} all-to-all(f32[32,40,128]{2,1,0:T(8,128)S(1)} %bitcast.23), channel_id=1, replica_groups=mesh['gx'=8,'gy'=4,'gz'=8] {'gx','gy'}, dimensions={0} | all-to-all | bytes 1310720 | tf_op jit(solution)/shard_map/all_to_all | solution.py:299
  210.9 10.7 %all_to_all.60 = f32[8,40,128]{2,1,0:T(8,128)S(1)} all-to-all(f32[8,40,128]{2,1,0:T(8,128)S(1)} %broadcast_in_dim.14), channel_id=1, replica_groups=mesh['gx'=8,'gy'=4,'gz'=8] {'gz'}, dimensions={0} | all-to-all | bytes 327680 | tf_op jit(solution)/shard_map/all_to_all | solution.py:299
  221.8 18.2 %all_to_all.61 = f32[32,40,128]{2,1,0:T(8,128)S(1)} all-to-all(f32[32,40,128]{2,1,0:T(8,128)S(1)} %broadcast_in_dim.15), channel_id=1, replica_groups=mesh['gx'=8,'gy'=4,'gz'=8] {'gx','gy'}, dimensions={0} | all-to-all | bytes 1310720 | tf_op jit(solution)/shard_map/all_to_all | solution.py:299
  240.0 13.1 %factor_two.1 = (f32[512,64]{1,0:T(8,128)S(1)}, f32[32,8,128]{2,1,0:T(8,128)S(1)}) custom-call(f32[10,128,128]{2,1,0:T(8,128)S(1)} %bitcast.20, f32[3,64,512]{2,1,0:T(8,128)S(1)} %bitcast.17, s32[3]{0:T(128)S(1)} %copy-done.5, f32[4,512,128]{2,1,0:T(8,128)S(1)} %get-tuple-element.16.a_ref), custom_call_target="tpu_custom_call" | custom-call | tf_op jit(solution)/shard_map/factor_two/pallas_call | solution.py:229
  253.1 12.0 %all_to_all.62 = f32[32,8,128]{2,1,0:T(8,128)S(1)} all-to-all(f32[32,8,128]{2,1,0:T(8,128)S(1)} %get-tuple-element.17), channel_id=1, replica_groups=mesh['gx'=8,'gy'=4,'gz'=8] {'gx','gy'}, dimensions={0} | all-to-all | bytes 262144 | tf_op jit(solution)/shard_map/all_to_all | solution.py:299
  265.2 31.1 %all_to_all.63.b_ref = f32[8,32,8,128]{3,2,1,0:T(8,128)S(1)} all-to-all(f32[8,32,8,128]{3,2,1,0:T(8,128)S(1)} %broadcast_in_dim.16), channel_id=1, replica_groups=mesh['gx'=8,'gy'=4,'gz'=8] {'gz'}, dimensions={0} | all-to-all | bytes 2097152 | tf_op jit(solution)/shard_map/all_to_all | solution.py:299
  296.3 0.8 gram_three.1
  297.2 16.3 %all_to_all.64 = f32[32,40,128]{2,1,0:T(8,128)S(1)} all-to-all(f32[32,40,128]{2,1,0:T(8,128)S(1)} %bitcast.21), channel_id=1, replica_groups=mesh['gx'=8,'gy'=4,'gz'=8] {'gx','gy'}, dimensions={0} | all-to-all | bytes 1310720 | tf_op jit(solution)/shard_map/all_to_all | solution.py:299
  313.5 0.9 broadcast_in_dim.17
  314.4 4.6 %all-to-all-start.10 = ((f32[32,40,128]{2,1,0:T(8,128)}), f32[32,40,128]{2,1,0:T(8,128)S(1)}, u32[]{:S(2)}, u32[]{:S(2)}) async-start(f32[32,40,128]{2,1,0:T(8,128)} %broadcast_in_dim.17), calls=%async_computation.10 | async-start | bytes 1310720 | tf_op jit(solution)/shard_map/all_to_all | solution.py:299
  319.0 12.5 %all-to-all-done.10 = f32[32,40,128]{2,1,0:T(8,128)S(1)} async-done(((f32[32,40,128]{2,1,0:T(8,128)}), f32[32,40,128]{2,1,0:T(8,128)S(1)}, u32[]{:S(2)}, u32[]{:S(2)}) %all-to-all-start.10) | async-done | bytes 655392 | tf_op jit(solution)/shard_map/all_to_all | solution.py:299
  331.5 12.7 %factor_three.1 = (f32[512,64]{1,0:T(8,128)S(1)}, f32[4,2,64,8]{3,2,1,0:T(8,128)S(1)}) custom-call(f32[10,128,128]{2,1,0:T(8,128)S(1)} %bitcast.22, f32[3,64,512]{2,1,0:T(8,128)S(1)} %bitcast.18, s32[3]{0:T(128)S(1)} %copy-done.5, s32[1]{0:T(128)} %bitcast.11.place_ref, f32[8,32,8,128]{3,2,1,0:T(8,128)S(1)} %all_to_all.63.b_ref), custom_call_target="tpu_custom_call" | custom-call | tf_op jit(solution)/shard_map/factor_three/pallas_call | solution.py:281
  344.3 1.0 copy.10
  (20 shorter events, 1.2 us)
Async XLA Ops:
  108.2 66.0 %copy-start.4 = (f32[3,512,64]{1,2,0:T(8,128)S(1)}, f32[3,512,64]{1,2,0:T(8,128)}, u32[]{:S(2)}) copy-start(f32[3,512,64]{1,2,0:T(8,128)} %param.4) | copy-start | bytes 1179652
  108.2 66.0 %copy-start.5 = (s32[3]{0:T(128)S(1)}, s32[3]{0:T(128)}, u32[]{:S(2)}) copy-start(s32[3]{0:T(128)} %rank_ref.5) | copy-start | bytes 40
  118.0 1.9 copy-start
  119.9 2.0 copy-start.2
  174.2 2.2 copy-start.1
  176.4 2.2 copy-start.3
  314.4 17.1 %all-to-all-start.10 = ((f32[32,40,128]{2,1,0:T(8,128)}), f32[32,40,128]{2,1,0:T(8,128)S(1)}, u32[]{:S(2)}, u32[]{:S(2)}) async-start(f32[32,40,128]{2,1,0:T(8,128)} %broadcast_in_dim.17), calls=%async_computation.10 | async-start | bytes 1310720 | tf_op jit(solution)/shard_map/all_to_all | solution.py:299

commit v2 on v1

v2 whole, which is shorter than its diff:
```python
import jax
import jax.numpy as jnp
from jax import lax
from jax.experimental import pallas as pl
from jax.experimental.pallas import tpu as pltpu
from jax.sharding import PartitionSpec as P

N = 512
R = 64
ITERS = 4
BF = jnp.bfloat16
F32 = jnp.float32
PAIRS = [(a, b) for a in range(4) for b in range(a, 4)]
NT = (((1,), (1,)), ((), ()))
NN = (((1,), (0,)), ((), ()))
VMEM = pl.BlockSpec(memory_space=pltpu.VMEM)
SMEM = pl.BlockSpec(memory_space=pltpu.SMEM)
HBM = pl.BlockSpec(memory_space=pltpu.HBM)


def split(x):
    hi = x.astype(BF)
    return hi, (x - hi.astype(F32)).astype(BF)


def mm(a, b, dims=NN):
    return lax.dot_general(a, b, dims, preferred_element_type=F32)


def put_blocks(keep_ref, send_ref, core, low, high):
    for here in range(2):

        @pl.when(core == here)
        def _():
            for n, (a, b) in enumerate(PAIRS):
                out_ref = keep_ref if n // 5 == here else send_ref
                if a < 2:
                    out_ref[n % 5] = low[a * 128 : a * 128 + 128, b * 128 : b * 128 + 128]
                else:
                    out_ref[n % 5] = high[a * 128 - 256 : a * 128 - 128, b * 128 - 256 : b * 128 - 128]


HALF = jax.ShapeDtypeStruct((5, 128, 128), F32)


def inverse_factor(cc):
    row8 = lax.broadcasted_iota(jnp.int32, (8, 128), 0)
    lane = lax.broadcasted_iota(jnp.int32, (8, 128), 1)
    m = [
        jnp.where(lane < R, (lane == row8 + 8 * b).astype(F32), cc[8 * b : 8 * b + 8, :])
        for b in range(8)
    ]
    scale = [jnp.ones((8, 128), F32) for _ in range(8)]
    for b0 in range(8):
        cols = [
            [jnp.broadcast_to(m[b][:, R + 8 * b0 + k : R + 8 * b0 + k + 1], (8, 128)) for b in range(b0, 8)]
            for k in range(8)
        ]
        for k in range(8):
            pivot = cols[k][0][k : k + 1, :]
            inv = 1.0 / pivot
            scaled_row = m[b0][k : k + 1, :] * inv
            factors = [cols[k2][0][k : k + 1, :] * inv for k2 in range(k + 1, 8)]
            scale[b0] = jnp.where(row8 == k, pivot, scale[b0])
            for b in range(b0, 8):
                c = cols[k][b - b0]
                if b == b0:
                    c = jnp.where(row8 > k, c, 0.0)
                m[b] = m[b] - c * scaled_row
                for k2 in range(k + 1, 8):
                    cols[k2][b - b0] = cols[k2][b - b0] - c * factors[k2 - k - 1]
    out = []
    for b in range(8):
        y = lax.rsqrt(scale[b])
        y = y * (1.5 - 0.5 * (scale[b] * y) * y)
        out.append(m[b] * y)
    return jnp.concatenate(out, axis=0)


def subspace(halves, core, start, gh_ref, gl_ref):
    for here in range(2):

        @pl.when(core == here)
        def _():
            for n, (a, b) in enumerate(PAIRS):
                blk = halves[(n // 5 + here) % 2][n % 5]
                hi, lo = split(blk)
                gh_ref[a * 128 : a * 128 + 128, b * 128 : b * 128 + 128] = hi
                gl_ref[a * 128 : a * 128 + 128, b * 128 : b * 128 + 128] = lo
                if a != b:
                    hi, lo = split(blk.T)
                    gh_ref[b * 128 : b * 128 + 128, a * 128 : a * 128 + 128] = hi
                    gl_ref[b * 128 : b * 128 + 128, a * 128 : a * 128 + 128] = lo

    lane = lax.broadcasted_iota(jnp.int32, (R, 128), 1)

    def image(vh, vs):
        t = mm(vs, gh_ref[...])
        return t[:R] + t[R:] + mm(vh, gl_ref[...])

    def step(k, w):
        wh, wl = split(w)
        ws = jnp.concatenate([wh, wl], axis=0)
        c = mm(ws, ws, NT)
        c = c[:R] + c[R:]
        z = jnp.where(k == ITERS - 1, w, image(wh, ws))
        zh, zl = split(z)
        li = inverse_factor(c + pltpu.roll(c, R, 1))
        lh = li.astype(BF).astype(F32)
        both = jnp.where(lane < R, lh, pltpu.roll(li - lh, R, 1)).astype(BF)
        return mm(
            jnp.concatenate([both, both], axis=1),
            jnp.concatenate([zh, zh, zl, zl], axis=0),
        )

    vh, vl = split(start)
    return lax.fori_loop(0, ITERS, step, image(vh, jnp.concatenate([vh, vl], axis=0)))


def masked_factor(halves, start_ref, rank_ref, place_ref, mode, gh_ref, gl_ref):
    v = subspace(halves, place_ref[0], start_ref[mode], gh_ref, gl_ref)
    row = lax.broadcasted_iota(jnp.int32, (R, N), 0)
    return jnp.where(row < rank_ref[mode], v, 0.0)


def gram_one_kernel(place_ref, x_ref, keep_ref, send_ref, x2_ref, low_ref, high_ref):
    step = pl.program_id(0)

    @pl.when(step == 0)
    def _():
        low_ref[...] = jnp.zeros_like(low_ref)
        high_ref[...] = jnp.zeros_like(high_ref)

    for p in range(8):
        for g in range(8):
            hi, lo = split(x_ref[g, 0, pl.ds(p, 64, stride=8), :])
            x2_ref[0, p, g * 64 : g * 64 + 64, :] = hi
            x2_ref[1, p, g * 64 : g * 64 + 64, :] = lo
    for p in range(0, 8, 4):
        xh = jnp.concatenate([x2_ref[0, p + k] for k in range(4)], axis=1)
        xl = jnp.concatenate([x2_ref[1, p + k] for k in range(4)], axis=1)
        low_ref[...] += mm(xh[:256], xh, NT) + mm(xh[:256], xl, NT) + mm(xl[:256], xh, NT)
        high_ref[...] += (
            mm(xh[256:], xh[256:], NT) + mm(xh[256:], xl[256:], NT) + mm(xl[256:], xh[256:], NT)
        )

    @pl.when(step == pl.num_programs(0) - 1)
    def _():
        put_blocks(keep_ref, send_ref, place_ref[0], low_ref[...] * 2.0**-20, high_ref[...] * 2.0**-20)


def gram_one(place, x):
    half = pl.BlockSpec((5, 128, 128), lambda i: (0, 0, 0))
    return pl.pallas_call(
        gram_one_kernel,
        grid=(4,),
        out_shape=(HALF, HALF, pltpu.HBM((2, 8, N, N), BF)),
        in_specs=[SMEM, pl.BlockSpec((8, 1, N, 128), lambda i: (0, i, 0, 0))],
        out_specs=(half, half, pl.BlockSpec((2, 8, N, 128), lambda i: (0, 0, 0, i))),
        scratch_shapes=[pltpu.VMEM((256, N), F32), pltpu.VMEM((256, 256), F32)],
        compiler_params=pltpu.CompilerParams(vmem_limit_bytes=40 * 2**20),
        name="gram_one",
    )(place, x)


def factor_one_kernel(
    mine_ref, other_ref, start_ref, rank_ref, place_ref, x_hbm, u_ref, a_ref, keep_ref, send_ref, gh_ref, gl_ref, x_ref, sem
):
    copy = pltpu.make_async_copy(x_hbm, x_ref, sem)
    copy.start()
    v = masked_factor((mine_ref, other_ref), start_ref, rank_ref, place_ref, 0, gh_ref, gl_ref)
    u_ref[...] = v
    vh, vl = split(v)
    vs = jnp.concatenate([vh, vl], axis=0)
    copy.wait()
    for p in range(8):
        t = mm(vs, x_ref[0, p])
        y = t[:R] + t[R:] + mm(vh, x_ref[1, p])
        for q in range(4):
            a_ref[q, pl.ds(p, R, stride=8), :] = y[:, 128 * q : 128 * q + 128]
    a = jnp.concatenate([a_ref[q] for q in range(4)], axis=1)
    ah, al = split(a)
    th, tl = split(a.T)
    low = mm(th[:256], ah) + mm(th[:256], al) + mm(tl[:256], ah)
    high = mm(th[256:], ah[:, 256:]) + mm(th[256:], al[:, 256:]) + mm(tl[256:], ah[:, 256:])
    put_blocks(keep_ref, send_ref, place_ref[0], low * 2.0**-20, high * 2.0**-20)


def factor_one(halves, starts, ranks, place, x2):
    return pl.pallas_call(
        factor_one_kernel,
        out_shape=(
            jax.ShapeDtypeStruct((R, N), F32),
            jax.ShapeDtypeStruct((4, N, 128), F32),
            HALF,
            HALF,
        ),
        in_specs=[VMEM, VMEM, VMEM, SMEM, SMEM, HBM],
        out_specs=(VMEM,) * 4,
        scratch_shapes=[
            pltpu.VMEM((N, N), BF),
            pltpu.VMEM((N, N), BF),
            pltpu.VMEM((2, 8, N, N), BF),
            pltpu.SemaphoreType.DMA,
        ],
        compiler_params=pltpu.CompilerParams(vmem_limit_bytes=53 * 2**20),
        name="factor_one",
    )(*halves, starts, ranks, place, x2)


def factor_two_kernel(mine_ref, other_ref, start_ref, rank_ref, place_ref, a_ref, u_ref, y_ref, gh_ref, gl_ref):
    v = masked_factor((mine_ref, other_ref), start_ref, rank_ref, place_ref, 1, gh_ref, gl_ref)
    u_ref[...] = v
    vh, vl = split(v)
    vs = jnp.concatenate([vh, vl], axis=0)
    ah, al = split(jnp.concatenate([a_ref[q] for q in range(4)], axis=1))
    y = mm(ah, vs, NT) + mm(al, vs, NT)
    y = y + pltpu.roll(y, R, 1)
    rolled = [y if k == 0 else pltpu.roll(y, 8 * k, 1) for k in range(8)]
    group = lax.broadcasted_iota(jnp.int32, (8, 128), 1) // 8
    for bx in range(8):
        for by in range(4):
            tile = jnp.zeros((8, 128), F32)
            for r in range(16):
                at = (by * 16 + r) * 8
                tile = jnp.where(group == r, rolled[(r - bx) % 8][at : at + 8, :], tile)
            y_ref[bx * 4 + by] = tile


def factor_two(halves, starts, ranks, place, a):
    return pl.pallas_call(
        factor_two_kernel,
        out_shape=(
            jax.ShapeDtypeStruct((R, N), F32),
            jax.ShapeDtypeStruct((32, 8, 128), F32),
        ),
        in_specs=[VMEM, VMEM, VMEM, SMEM, SMEM, VMEM],
        out_specs=(VMEM, VMEM),
        scratch_shapes=[pltpu.VMEM((N, N), BF), pltpu.VMEM((N, N), BF)],
        compiler_params=pltpu.CompilerParams(vmem_limit_bytes=32 * 2**20),
        name="factor_two",
    )(*halves, starts, ranks, place, a)


def pack_kernel(y_ref, out_ref):
    group = lax.broadcasted_iota(jnp.int32, (32, 128), 1) // 16
    for z in range(8):
        rows = jnp.zeros((32, 128), F32)
        for g in range(8):
            at = 8 * (g % 4) + 4 * (g // 4)
            tile = y_ref[at : at + 4].reshape(32, 128)
            if g != z:
                tile = pltpu.roll(tile, (16 * (g - z)) % 128, 1)
            rows = jnp.where(group == g, tile, rows)
        out_ref[z] = rows


def pack(y):
    return pl.pallas_call(
        pack_kernel,
        out_shape=jax.ShapeDtypeStruct((8, 32, 128), F32),
        in_specs=[VMEM],
        out_specs=VMEM,
        name="pack",
    )(y)


def gram_three_kernel(place_ref, y_ref, keep_ref, send_ref, b_ref):
    lane = lax.broadcasted_iota(jnp.int32, (32, 128), 1)
    for z in range(8):
        y = y_ref[z]
        b_ref[64 * z : 64 * z + 32, :] = jnp.where(lane < R, y, 0.0)
        b_ref[64 * z + 32 : 64 * z + 64, :] = jnp.where(lane < R, pltpu.roll(y, R, 1), 0.0)
    bh, bl = split(b_ref[...])
    low = mm(bh[:256], bh, NT) + mm(bh[:256], bl, NT) + mm(bl[:256], bh, NT)
    high = mm(bh[256:], bh[256:], NT) + mm(bh[256:], bl[256:], NT) + mm(bl[256:], bh[256:], NT)
    put_blocks(keep_ref, send_ref, place_ref[0], low * 2.0**-20, high * 2.0**-20)


def gram_three(place, y):
    return pl.pallas_call(
        gram_three_kernel,
        out_shape=(HALF, HALF, jax.ShapeDtypeStruct((N, 128), F32)),
        in_specs=[SMEM, VMEM],
        out_specs=(VMEM, VMEM, VMEM),
        compiler_params=pltpu.CompilerParams(vmem_limit_bytes=32 * 2**20),
        name="gram_three",
    )(place, y)


def factor_three_kernel(
    mine_ref, other_ref, start_ref, rank_ref, place_ref, b_ref, u_one_ref, u_two_ref, u_ref, core_ref, gh_ref, gl_ref
):
    v = masked_factor((mine_ref, other_ref), start_ref, rank_ref, place_ref, 2, gh_ref, gl_ref)
    u_ref[0] = u_one_ref[...]
    u_ref[1] = u_two_ref[...]
    u_ref[2] = v
    vh, vl = split(v)
    bh, bl = split(b_ref[...])
    t = mm(jnp.concatenate([vh, vl], axis=0), bh)
    core = t[:R] + t[R:] + mm(vh, bl)
    core = jnp.concatenate([core, core], axis=0).T
    for s in range(4):
        for e in range(2):
            core_ref[s, e] = core[16 * s + 8 * e : 16 * s + 8 * e + 8, :R]


def factor_three(halves, starts, ranks, place, b, u_one, u_two):
    return pl.pallas_call(
        factor_three_kernel,
        out_shape=(
            jax.ShapeDtypeStruct((3, R, N), F32),
            jax.ShapeDtypeStruct((4, 2, 8, R), F32),
        ),
        in_specs=[VMEM, VMEM, VMEM, SMEM, SMEM, VMEM, VMEM, VMEM],
        out_specs=(VMEM, VMEM),
        scratch_shapes=[pltpu.VMEM((N, N), BF), pltpu.VMEM((N, N), BF)],
        compiler_params=pltpu.CompilerParams(vmem_limit_bytes=32 * 2**20),
        name="factor_three",
    )(*halves, starts, ranks, place, b, u_one, u_two)


PLANE = ("y", "gy")


def swap(x, axes):
    return lax.all_to_all(x, axes, 0, 0, tiled=True)


def spread(x, axes, count):
    return swap(jnp.broadcast_to(x[None], (count,) + x.shape), axes)


def other_core(x):
    return lax.ppermute(x, "core", [(0, 1), (1, 0)])


def total(keep, send):
    g = keep + other_core(send)
    g = jnp.sum(swap(g.reshape(16, 40, 128), PLANE), axis=0)
    g = jnp.sum(spread(g, "gz", 8), axis=0)
    g = spread(g, PLANE, 16).reshape(5, 128, 128)
    return g, other_core(g)


def local(tensor, starts, trunc_ranks):
    starts_t = jnp.swapaxes(starts, 1, 2)
    place = lax.axis_index("core").astype(jnp.int32).reshape(1)
    tensor, place = lax.optimization_barrier((tensor, place))
    x = tensor.reshape(4, 64, 8, 8, 128).transpose(0, 2, 1, 3, 4).reshape(32, N, 128)
    x = swap(x, ("y", "core", "gy")).reshape(8, 4, N, 128)
    keep, send, x2 = gram_one(place, x)
    u_one, a, keep, send = factor_one(total(keep, send), starts_t, trunc_ranks, place, x2)
    u_two, y = factor_two(total(keep, send), starts_t, trunc_ranks, place, a)
    y = pack(swap(y, ("y", "core", "gy")))
    keep, send, b = gram_three(place, swap(y, "gz"))
    factors, core_out = factor_three(total(keep, send), starts_t, trunc_ranks, place, b, u_one, u_two)
    return (jnp.swapaxes(core_out, 2, 3), jnp.swapaxes(factors, 1, 2))


def solution(mesh):
    fine = jax.sharding.Mesh(mesh.devices.reshape(4, 2, 4, 8), ("y", "core", "gy", "gz"))
    gx = ("y", "core")
    return jax.shard_map(
        local,
        mesh=fine,
        in_specs=(P(None, gx, "gz", "gy"), P(), P()),
        out_specs=(P(None, ("gy", "gz"), None, gx), P()),
        check_vma=False,
    )
```

time: 347 us -> 307 us (0.88)
  blocking collectives: 261 us -> 231 us
  starting transfers between devices: 4.57 us -> 15 us
  local copies, waits for them, and re-layouts: 15.5 us -> 6.5 us
  Pallas kernels: 51.7 us -> 44.6 us
  waiting for transfers between devices: 12.5 us -> 7.54 us
    all_to_all x10 -> x12, blocking collectives: 261 us -> 231 us  [swap(): return lax.all_to_all(x, axes, 0, 0, tiled=True)]
    ppermute x0 -> x6, starting transfers between devices: none -> 15 us  [other_core(): return lax.ppermute(x, 'core', [(0, 1), (1, 0)])]
    all_to_all x1 -> x0, waiting for transfers between devices: 12.5 us -> none  [swap(): return lax.all_to_all(x, axes, 0, 0, tiled=True)]
    unnamed x14 -> x10, local copies, waits for them, and re-layouts: 10 us -> 1.96 us
    ppermute x0 -> x6, waiting for transfers between devices: none -> 7.54 us  [other_core(): return lax.ppermute(x, 'core', [(0, 1), (1, 0)])]
    pallas_call x5 -> x6, Pallas kernels: 51.7 us -> 44.6 us  [the longest x1 13.3 us: factor_one(): pl.pallas_call(factor_one_kernel, out_shape=(jax.ShapeDtypeStruct((R, N),...]
    all_to_all x1 -> x0, starting transfers between devices: 4.57 us -> none  [swap(): return lax.all_to_all(x, axes, 0, 0, tiled=True)]
  transfers between devices with their start and end apart: 1 -> 6, of which waited for: 1 -> 6; matrix products, arithmetic and copies ran while one was open for 0% -> 0% of each run, Pallas kernels for 0% -> 0%
where the time goes in v2:
time: 307 us; the launch traced here: 306 us
  blocking collectives  231 us (75%)
  Pallas kernels  44.6 us (15%)
  starting transfers between devices  15 us (5%)
  waiting for transfers between devices  7.54 us (2%)
  local copies, waits for them, and re-layouts  6.5 us (2%)
    all_to_all x12, blocking collectives, swap(): return lax.all_to_all(x, axes, 0, 0, tiled=True)  231 us
    ppermute x6, starting transfers between devices, other_core(): return lax.ppermute(x, 'core', [(0, 1), (1, 0)])  15 us
    pallas_call x1, Pallas kernels, factor_one(): pl.pallas_call(factor_one_kernel, out_shape=(jax.ShapeDtypeStruct((R, N),...  13.3 us
    pallas_call x1, Pallas kernels, factor_two(): pl.pallas_call(factor_two_kernel, out_shape=(jax.ShapeDtypeStruct((R, N),...  10.2 us
    pallas_call x1, Pallas kernels, factor_three(): pl.pallas_call(factor_three_kernel, out_shape=(jax.ShapeDtypeStruct((3, R...  10 us
    pallas_call x1, Pallas kernels, gram_one(): pl.pallas_call(gram_one_kernel, grid=(4,), out_shape=(HALF, HALF, pltpu.H...  8.63 us
    ppermute x6, waiting for transfers between devices, other_core(): return lax.ppermute(x, 'core', [(0, 1), (1, 0)])  7.54 us
  transfers between devices with their start and end apart: 6, of which 6 were waited for; matrix products, arithmetic and copies ran while one was open for 0% of the time, Pallas kernels for 0%

profile of v2, /device:TPU:1, one launch (start us, length us, event | category | flops | bytes accessed | tf_op | source)
XLA Modules:
  0.0 306.1 jit_solution(8171658785127366622)
XLA Ops:
  0.6 4.4 %copy.6 = f32[4,8,64,8,128]{4,3,2,1,0:T(8,128)S(1)} copy(f32[4,8,64,8,128]{4,3,1,2,0:T(8,128)} %bitcast.24) | data formatting | bytes 16777216 | tf_op jit(solution)/shard_map/transpose | solution.py:350
  5.1 103.1 %all_to_all.60 = f32[32,512,128]{2,1,0:T(8,128)S(1)} all-to-all(f32[32,512,128]{2,1,0:T(8,128)S(1)} %bitcast.23), channel_id=1, replica_groups=mesh['y'=4,'core'=2,'gy'=4,'gz'=8] {'y','core','gy'}, dimensions={0} | all-to-all | bytes 16777216 | tf_op jit(solution)/shard_map/all_to_all | solution.py:327
  108.1 8.6 %gram_one.1 = (f32[5,128,128]{2,1,0:T(8,128)S(1)}, f32[5,128,128]{2,1,0:T(8,128)S(1)}, bf16[2,8,512,512]{3,2,1,0:T(8,128)(2,1)}) custom-call(s32[1]{0:T(128)} %bitcast.place_ref, f32[8,4,512,128]{3,2,1,0:T(8,128)S(1)} %bitcast.15), custom_call_target="tpu_custom_call" | custom-call | tf_op jit(solution)/shard_map/gram_one/pallas_call | solution.py:154
  116.8 1.3 collective-permute-start
  119.3 12.4 %all_to_all.61 = f32[16,40,128]{2,1,0:T(8,128)S(1)} all-to-all(f32[16,40,128]{2,1,0:T(8,128)S(1)} %bitcast.27), channel_id=1, replica_groups=mesh['y'=4,'core'=2,'gy'=4,'gz'=8] {'y','gy'}, dimensions={0} | all-to-all | bytes 655360 | tf_op jit(solution)/shard_map/all_to_all | solution.py:327
  131.8 16.3 %all_to_all.62 = f32[8,40,128]{2,1,0:T(8,128)S(1)} all-to-all(f32[8,40,128]{2,1,0:T(8,128)S(1)} %broadcast_in_dim.12), channel_id=1, replica_groups=mesh['y'=4,'core'=2,'gy'=4,'gz'=8] {'gz'}, dimensions={0} | all-to-all | bytes 327680 | tf_op jit(solution)/shard_map/all_to_all | solution.py:327
  148.1 10.9 %all_to_all.63 = f32[16,40,128]{2,1,0:T(8,128)S(1)} all-to-all(f32[16,40,128]{2,1,0:T(8,128)S(1)} %broadcast_in_dim.13), channel_id=1, replica_groups=mesh['y'=4,'core'=2,'gy'=4,'gz'=8] {'y','gy'}, dimensions={0} | all-to-all | bytes 655360 | tf_op jit(solution)/shard_map/all_to_all | solution.py:327
  159.1 3.9 %collective-permute-start.1 = (f32[5,128,128]{2,1,0:T(8,128)S(1)}, f32[5,128,128]{2,1,0:T(8,128)S(1)}, u32[]{:S(2)}, u32[]{:S(2)}) collective-permute-start(f32[5,128,128]{2,1,0:T(8,128)S(1)} %bitcast.25), channel_id=1, source_target_pairs={{0,32},{32,0},{1,33},{33,1},{2,34},{34,2},{3,35},{35,3},{4,36},{36... | collective-permute-start | bytes 983048 | tf_op jit(solution)/shard_map/ppermute | solution.py:335
  165.0 13.3 %factor_one.1 = (f32[64,512]{1,0:T(8,128)S(1)}, f32[4,512,128]{2,1,0:T(8,128)}, f32[5,128,128]{2,1,0:T(8,128)S(1)}, f32[5,128,128]{2,1,0:T(8,128)S(1)}) custom-call(f32[5,128,128]{2,1,0:T(8,128)} %bitcast.26, f32[5,128,128]{2,1,0:T(8,128)} %copy-done.4, f32[3,64,512]{2,1,0:T(8,128)} %bitcast.16, s32[3]{0:T(128)S(1)} %copy-done.2, s32[1]{0:T(128)} %bitcast.place_ref, ...), custom_call_target="tpu_custom_call" | custom-call | tf_op jit(solution)/shard_map/factor_one/pallas_call | solution.py:190
  178.7 1.3 collective-permute-done.2
  180.1 11.4 %all_to_all.64 = f32[16,40,128]{2,1,0:T(8,128)S(1)} all-to-all(f32[16,40,128]{2,1,0:T(8,128)S(1)} %bitcast.28), channel_id=1, replica_groups=mesh['y'=4,'core'=2,'gy'=4,'gz'=8] {'y','gy'}, dimensions={0} | all-to-all | bytes 655360 | tf_op jit(solution)/shard_map/all_to_all | solution.py:327
  191.5 10.8 %all_to_all.65 = f32[8,40,128]{2,1,0:T(8,128)S(1)} all-to-all(f32[8,40,128]{2,1,0:T(8,128)S(1)} %broadcast_in_dim.14), channel_id=1, replica_groups=mesh['y'=4,'core'=2,'gy'=4,'gz'=8] {'gz'}, dimensions={0} | all-to-all | bytes 327680 | tf_op jit(solution)/shard_map/all_to_all | solution.py:327
  202.4 10.5 %all_to_all.66 = f32[16,40,128]{2,1,0:T(8,128)S(1)} all-to-all(f32[16,40,128]{2,1,0:T(8,128)S(1)} %broadcast_in_dim.15), channel_id=1, replica_groups=mesh['y'=4,'core'=2,'gy'=4,'gz'=8] {'y','gy'}, dimensions={0} | all-to-all | bytes 655360 | tf_op jit(solution)/shard_map/all_to_all | solution.py:327
  212.9 3.9 %collective-permute-start.3 = (f32[5,128,128]{2,1,0:T(8,128)S(1)}, f32[5,128,128]{2,1,0:T(8,128)S(1)}, u32[]{:S(2)}, u32[]{:S(2)}) collective-permute-start(f32[5,128,128]{2,1,0:T(8,128)S(1)} %bitcast.21), channel_id=1, source_target_pairs={{0,32},{32,0},{1,33},{33,1},{2,34},{34,2},{3,35},{35,3},{4,36},{36... | collective-permute-start | bytes 983048 | tf_op jit(solution)/shard_map/ppermute | solution.py:335
  219.3 10.2 %factor_two.1 = (f32[64,512]{1,0:T(8,128)S(1)}, f32[32,8,128]{2,1,0:T(8,128)S(1)}) custom-call(f32[5,128,128]{2,1,0:T(8,128)S(1)} %bitcast.22, f32[5,128,128]{2,1,0:T(8,128)S(1)} %collective-permute-done.3.other_ref, f32[3,64,512]{2,1,0:T(8,128)S(1)} %bitcast.17, s32[3]{0:T(128)S(1)} %copy-done.2, s32[1]{0:T(128)} %bitcast.place_ref, ...), custom_call_target="tpu_custom_call" | custom-call | tf_op jit(solution)/shard_map/factor_two/pallas_call | solution.py:231
  229.5 11.4 %all_to_all.67.y_ref = f32[32,8,128]{2,1,0:T(8,128)} all-to-all(f32[32,8,128]{2,1,0:T(8,128)S(1)} %get-tuple-element.26), channel_id=1, replica_groups=mesh['y'=4,'core'=2,'gy'=4,'gz'=8] {'y','core','gy'}, dimensions={0} | all-to-all | bytes 262144 | tf_op jit(solution)/shard_map/all_to_all | solution.py:327
  240.9 1.9 pack.1
  242.8 11.8 %all_to_all.68.y_ref = f32[8,32,128]{2,1,0:T(8,128)S(1)} all-to-all(f32[8,32,128]{2,1,0:T(8,128)} %pack.1), channel_id=1, replica_groups=mesh['y'=4,'core'=2,'gy'=4,'gz'=8] {'gz'}, dimensions={0} | all-to-all | bytes 262144 | tf_op jit(solution)/shard_map/all_to_all | solution.py:327
  255.1 1.6 collective-permute-start.4
  258.0 11.5 %all_to_all.69 = f32[16,40,128]{2,1,0:T(8,128)S(1)} all-to-all(f32[16,40,128]{2,1,0:T(8,128)S(1)} %bitcast.29), channel_id=1, replica_groups=mesh['y'=4,'core'=2,'gy'=4,'gz'=8] {'y','gy'}, dimensions={0} | all-to-all | bytes 655360 | tf_op jit(solution)/shard_map/all_to_all | solution.py:327
  269.6 10.7 %all_to_all.70 = f32[8,40,128]{2,1,0:T(8,128)S(1)} all-to-all(f32[8,40,128]{2,1,0:T(8,128)S(1)} %broadcast_in_dim.16), channel_id=1, replica_groups=mesh['y'=4,'core'=2,'gy'=4,'gz'=8] {'gz'}, dimensions={0} | all-to-all | bytes 327680 | tf_op jit(solution)/shard_map/all_to_all | solution.py:327
  280.4 10.6 %all_to_all.71 = f32[16,40,128]{2,1,0:T(8,128)S(1)} all-to-all(f32[16,40,128]{2,1,0:T(8,128)S(1)} %broadcast_in_dim.17), channel_id=1, replica_groups=mesh['y'=4,'core'=2,'gy'=4,'gz'=8] {'y','gy'}, dimensions={0} | all-to-all | bytes 655360 | tf_op jit(solution)/shard_map/all_to_all | solution.py:327
  290.9 3.9 %collective-permute-start.5 = (f32[5,128,128]{2,1,0:T(8,128)S(1)}, f32[5,128,128]{2,1,0:T(8,128)S(1)}, u32[]{:S(2)}, u32[]{:S(2)}) collective-permute-start(f32[5,128,128]{2,1,0:T(8,128)S(1)} %bitcast.19), channel_id=1, source_target_pairs={{0,32},{32,0},{1,33},{33,1},{2,34},{34,2},{3,35},{35,3},{4,36},{36... | collective-permute-start | bytes 983048 | tf_op jit(solution)/shard_map/ppermute | solution.py:335
  296.1 10.0 %factor_three.1 = (f32[3,64,512]{2,1,0:T(8,128)}, f32[4,2,8,64]{3,2,1,0:T(8,128)}) custom-call(f32[5,128,128]{2,1,0:T(8,128)S(1)} %bitcast.20, f32[5,128,128]{2,1,0:T(8,128)S(1)} %collective-permute-done.5.other_ref, f32[3,64,512]{2,1,0:T(8,128)S(1)} %bitcast.18, s32[3]{0:T(128)S(1)} %copy-done.2, s32[1]{0:T(128)} %bitcast.place_ref, ...), custom_call_target="tpu_custom_call" | custom-call | tf_op jit(solution)/shard_map/factor_three/pallas_call | solution.py:309
  (32 shorter events, 9.6 us)
Async XLA Ops:
  108.1 56.8 %copy-start.2 = (s32[3]{0:T(128)S(1)}, s32[3]{0:T(128)}, u32[]{:S(2)}) copy-start(s32[3]{0:T(128)} %rank_ref.5) | copy-start | bytes 40
  116.8 2.5 collective-permute-start
  119.3 98.8 %copy-start = (f32[3,512,64]{1,2,0:T(8,128)S(1)}, f32[3,512,64]{1,2,0:T(8,128)}, u32[]{:S(2)}) copy-start(f32[3,512,64]{1,2,0:T(8,128)} %param.4) | copy-start | bytes 1179652
  159.1 5.2 %copy-start.3 = (f32[16,40,128]{2,1,0:T(8,128)}, f32[16,40,128]{2,1,0:T(8,128)S(1)}, u32[]{:S(2)}) copy-start(f32[16,40,128]{2,1,0:T(8,128)S(1)} %all_to_all.63) | copy-start | bytes 983044
  159.1 5.2 %collective-permute-start.1 = (f32[5,128,128]{2,1,0:T(8,128)S(1)}, f32[5,128,128]{2,1,0:T(8,128)S(1)}, u32[]{:S(2)}, u32[]{:S(2)}) collective-permute-start(f32[5,128,128]{2,1,0:T(8,128)S(1)} %bitcast.25), channel_id=1, source_target_pairs={{0,32},{32,0},{1,33},{33,1},{2,34},{34,2},{3,35},{35,3},{4,36},{36... | collective-permute-start | bytes 983048 | tf_op jit(solution)/shard_map/ppermute | solution.py:335
  164.2 0.7 copy-start.4
  178.3 1.7 collective-permute-start.2
  212.9 5.2 %collective-permute-start.3 = (f32[5,128,128]{2,1,0:T(8,128)S(1)}, f32[5,128,128]{2,1,0:T(8,128)S(1)}, u32[]{:S(2)}, u32[]{:S(2)}) collective-permute-start(f32[5,128,128]{2,1,0:T(8,128)S(1)} %bitcast.21), channel_id=1, source_target_pairs={{0,32},{32,0},{1,33},{33,1},{2,34},{34,2},{3,35},{35,3},{4,36},{36... | collective-permute-start | bytes 983048 | tf_op jit(solution)/shard_map/ppermute | solution.py:335
  218.1 1.2 copy-start.1
  255.1 2.9 collective-permute-start.4
  290.9 5.2 %collective-permute-start.5 = (f32[5,128,128]{2,1,0:T(8,128)S(1)}, f32[5,128,128]{2,1,0:T(8,128)S(1)}, u32[]{:S(2)}, u32[]{:S(2)}) collective-permute-start(f32[5,128,128]{2,1,0:T(8,128)S(1)} %bitcast.19), channel_id=1, source_target_pairs={{0,32},{32,0},{1,33},{33,1},{2,34},{34,2},{3,35},{35,3},{4,36},{36... | collective-permute-start | bytes 983048 | tf_op jit(solution)/shard_map/ppermute | solution.py:335

commit v3 on v2

--- a/solution.py
+++ b/solution.py
@@ -43,6 +43,14 @@
 HALF = jax.ShapeDtypeStruct((5, 128, 128), F32)
 
 
+def column(x, j):
+    return jnp.broadcast_to(x[:, R + j : R + j + 1], (8, 128))
+
+
+def row(x, k):
+    return jnp.broadcast_to(x[k : k + 1, :], (8, 128))
+
+
 def inverse_factor(cc):
     row8 = lax.broadcasted_iota(jnp.int32, (8, 128), 0)
     lane = lax.broadcasted_iota(jnp.int32, (8, 128), 1)
@@ -50,25 +58,30 @@
         jnp.where(lane < R, (lane == row8 + 8 * b).astype(F32), cc[8 * b : 8 * b + 8, :])
         for b in range(8)
     ]
-    scale = [jnp.ones((8, 128), F32) for _ in range(8)]
+    scale = []
+    diag = [column(m[0], k) for k in range(8)]
     for b0 in range(8):
-        cols = [
-            [jnp.broadcast_to(m[b][:, R + 8 * b0 + k : R + 8 * b0 + k + 1], (8, 128)) for b in range(b0, 8)]
-            for k in range(8)
-        ]
+        below = [[column(m[b], 8 * b0 + k) for b in range(b0 + 1, 8)] for k in range(8)]
+        ahead = [column(m[b0 + 1], 8 * b0 + 8 + k) for k in range(8)] if b0 < 7 else []
+        pivots = jnp.ones((8, 128), F32)
         for k in range(8):
-            pivot = cols[k][0][k : k + 1, :]
+            pivot = row(diag[k], k)
             inv = 1.0 / pivot
-            scaled_row = m[b0][k : k + 1, :] * inv
-            factors = [cols[k2][0][k : k + 1, :] * inv for k2 in range(k + 1, 8)]
-            scale[b0] = jnp.where(row8 == k, pivot, scale[b0])
-            for b in range(b0, 8):
-                c = cols[k][b - b0]
-                if b == b0:
-                    c = jnp.where(row8 > k, c, 0.0)
-                m[b] = m[b] - c * scaled_row
-                for k2 in range(k + 1, 8):
-                    cols[k2][b - b0] = cols[k2][b - b0] - c * factors[k2 - k - 1]
+            scaled_row = row(m[b0], k) * inv
+            rest = jnp.where(row8 > k, diag[k], 0.0)
+            pivots = jnp.where(row8 == k, pivot, pivots)
+            factors = {k2: row(diag[k2], k) * inv for k2 in range(k + 1, 8)}
+            for k2 in factors:
+                diag[k2] = diag[k2] - rest * factors[k2]
+            m[b0] = m[b0] - rest * scaled_row
+            for n in range(7 - b0):
+                m[b0 + 1 + n] = m[b0 + 1 + n] - below[k][n] * scaled_row
+                for k2 in factors:
+                    below[k2][n] = below[k2][n] - below[k][n] * factors[k2]
+            for k2 in range(len(ahead)):
+                ahead[k2] = ahead[k2] - below[k][0] * (row(below[k][0], k2) * inv)
+        scale.append(pivots)
+        diag = ahead
     out = []
     for b in range(8):
         y = lax.rsqrt(scale[b])
@@ -119,17 +132,18 @@
 
 def masked_factor(halves, start_ref, rank_ref, place_ref, mode, gh_ref, gl_ref):
     v = subspace(halves, place_ref[0], start_ref[mode], gh_ref, gl_ref)
-    row = lax.broadcasted_iota(jnp.int32, (R, N), 0)
-    return jnp.where(row < rank_ref[mode], v, 0.0)
-
-
-def gram_one_kernel(place_ref, x_ref, keep_ref, send_ref, x2_ref, low_ref, high_ref):
+    index = lax.broadcasted_iota(jnp.int32, (R, N), 0)
+    return jnp.where(index < rank_ref[mode], v, 0.0)
+
+
+def gram_one_kernel(place_ref, x_ref, keep_ref, send_ref, x2_ref, low_ref, high_ref, cross_ref):
     step = pl.program_id(0)
 
     @pl.when(step == 0)
     def _():
         low_ref[...] = jnp.zeros_like(low_ref)
         high_ref[...] = jnp.zeros_like(high_ref)
+        cross_ref[...] = jnp.zeros_like(cross_ref)
 
     for p in range(8):
         for g in range(8):
@@ -139,14 +153,17 @@
     for p in range(0, 8, 4):
         xh = jnp.concatenate([x2_ref[0, p + k] for k in range(4)], axis=1)
         xl = jnp.concatenate([x2_ref[1, p + k] for k in range(4)], axis=1)
-        low_ref[...] += mm(xh[:256], xh, NT) + mm(xh[:256], xl, NT) + mm(xl[:256], xh, NT)
-        high_ref[...] += (
-            mm(xh[256:], xh[256:], NT) + mm(xh[256:], xl[256:], NT) + mm(xl[256:], xh[256:], NT)
-        )
+        low_ref[...] += mm(xh[:256], xh, NT)
+        high_ref[...] += mm(xh[256:], xh[256:], NT)
+        cross_ref[...] += mm(xh, xl, NT)
 
     @pl.when(step == pl.num_programs(0) - 1)
     def _():
-        put_blocks(keep_ref, send_ref, place_ref[0], low_ref[...] * 2.0**-20, high_ref[...] * 2.0**-20)
+        cross = cross_ref[...]
+        cross = cross + cross.T
+        low = low_ref[...] + cross[:256]
+        high = high_ref[...] + cross[256:, 256:]
+        put_blocks(keep_ref, send_ref, place_ref[0], low * 2.0**-20, high * 2.0**-20)
 
 
 def gram_one(place, x):
@@ -157,7 +174,7 @@
         out_shape=(HALF, HALF, pltpu.HBM((2, 8, N, N), BF)),
         in_specs=[SMEM, pl.BlockSpec((8, 1, N, 128), lambda i: (0, i, 0, 0))],
         out_specs=(half, half, pl.BlockSpec((2, 8, N, 128), lambda i: (0, 0, 0, i))),
-        scratch_shapes=[pltpu.VMEM((256, N), F32), pltpu.VMEM((256, 256), F32)],
+        scratch_shapes=[pltpu.VMEM((256, N), F32), pltpu.VMEM((256, 256), F32), pltpu.VMEM((N, N), F32)],
         compiler_params=pltpu.CompilerParams(vmem_limit_bytes=40 * 2**20),
         name="gram_one",
     )(place, x)
@@ -203,7 +220,7 @@
             pltpu.VMEM((2, 8, N, N), BF),
             pltpu.SemaphoreType.DMA,
         ],
-        compiler_params=pltpu.CompilerParams(vmem_limit_bytes=53 * 2**20),
+        compiler_params=pltpu.CompilerParams(vmem_limit_bytes=48 * 2**20),
         name="factor_one",
     )(*halves, starts, ranks, place, x2)
 

time: 307 us -> 300 us (0.977)
  Pallas kernels: 44.6 us -> 39.6 us
where the time goes in v3:
time: 300 us; the launch traced here: 299 us
  blocking collectives  231 us (77%)
  Pallas kernels  39.6 us (13%)
  starting transfers between devices  15 us (5%)
  waiting for transfers between devices  7.54 us (3%)
  local copies, waits for them, and re-layouts  4.55 us (2%)
    all_to_all x12, blocking collectives, swap(): return lax.all_to_all(x, axes, 0, 0, tiled=True)  231 us
    ppermute x6, starting transfers between devices, other_core(): return lax.ppermute(x, 'core', [(0, 1), (1, 0)])  15 us
    pallas_call x1, Pallas kernels, factor_one(): pl.pallas_call(factor_one_kernel, out_shape=(jax.ShapeDtypeStruct((R, N),...  10.7 us
    pallas_call x1, Pallas kernels, factor_two(): pl.pallas_call(factor_two_kernel, out_shape=(jax.ShapeDtypeStruct((R, N),...  9.28 us
    pallas_call x1, Pallas kernels, factor_three(): pl.pallas_call(factor_three_kernel, out_shape=(jax.ShapeDtypeStruct((3, R...  9.1 us
    pallas_call x1, Pallas kernels, gram_one(): pl.pallas_call(gram_one_kernel, grid=(4,), out_shape=(HALF, HALF, pltpu.H...  8.1 us
    ppermute x6, waiting for transfers between devices, other_core(): return lax.ppermute(x, 'core', [(0, 1), (1, 0)])  7.54 us
  transfers between devices with their start and end apart: 6, of which 6 were waited for; matrix products, arithmetic and copies ran while one was open for 0% of the time, Pallas kernels for 0%

profile of v3, /device:TPU:1, one launch (start us, length us, event | category | flops | bytes accessed | tf_op | source)
XLA Modules:
  0.0 299.0 jit_solution(17531432830534690963)
XLA Ops:
  0.6 4.4 %copy.6 = f32[4,8,64,8,128]{4,3,2,1,0:T(8,128)S(1)} copy(f32[4,8,64,8,128]{4,3,1,2,0:T(8,128)} %bitcast.26) | data formatting | bytes 16777216 | tf_op jit(solution)/shard_map/transpose | solution.py:367
  5.1 103.1 %all_to_all.60 = f32[32,512,128]{2,1,0:T(8,128)S(1)} all-to-all(f32[32,512,128]{2,1,0:T(8,128)S(1)} %bitcast.25), channel_id=1, replica_groups=mesh['y'=4,'core'=2,'gy'=4,'gz'=8] {'y','core','gy'}, dimensions={0} | all-to-all | bytes 16777216 | tf_op jit(solution)/shard_map/all_to_all | solution.py:344
  108.1 8.1 %gram_one.1 = (f32[5,128,128]{2,1,0:T(8,128)S(1)}, f32[5,128,128]{2,1,0:T(8,128)S(1)}, bf16[2,8,512,512]{3,2,1,0:T(8,128)(2,1)}) custom-call(s32[1]{0:T(128)} %bitcast.place_ref, f32[8,4,512,128]{3,2,1,0:T(8,128)S(1)} %bitcast.15), custom_call_target="tpu_custom_call" | custom-call | tf_op jit(solution)/shard_map/gram_one/pallas_call | solution.py:171
  116.2 1.3 collective-permute-start
  118.8 12.3 %all_to_all.61 = f32[16,40,128]{2,1,0:T(8,128)S(1)} all-to-all(f32[16,40,128]{2,1,0:T(8,128)S(1)} %bitcast.27), channel_id=1, replica_groups=mesh['y'=4,'core'=2,'gy'=4,'gz'=8] {'y','gy'}, dimensions={0} | all-to-all | bytes 655360 | tf_op jit(solution)/shard_map/all_to_all | solution.py:344
  131.1 16.3 %all_to_all.62 = f32[8,40,128]{2,1,0:T(8,128)S(1)} all-to-all(f32[8,40,128]{2,1,0:T(8,128)S(1)} %broadcast_in_dim.12), channel_id=1, replica_groups=mesh['y'=4,'core'=2,'gy'=4,'gz'=8] {'gz'}, dimensions={0} | all-to-all | bytes 327680 | tf_op jit(solution)/shard_map/all_to_all | solution.py:344
  147.5 10.9 %all_to_all.63 = f32[16,40,128]{2,1,0:T(8,128)S(1)} all-to-all(f32[16,40,128]{2,1,0:T(8,128)S(1)} %broadcast_in_dim.13), channel_id=1, replica_groups=mesh['y'=4,'core'=2,'gy'=4,'gz'=8] {'y','gy'}, dimensions={0} | all-to-all | bytes 655360 | tf_op jit(solution)/shard_map/all_to_all | solution.py:344
  158.4 3.9 %collective-permute-start.1 = (f32[5,128,128]{2,1,0:T(8,128)S(1)}, f32[5,128,128]{2,1,0:T(8,128)S(1)}, u32[]{:S(2)}, u32[]{:S(2)}) collective-permute-start(f32[5,128,128]{2,1,0:T(8,128)S(1)} %bitcast.19), channel_id=1, source_target_pairs={{0,32},{32,0},{1,33},{33,1},{2,34},{34,2},{3,35},{35,3},{4,36},{36... | collective-permute-start | bytes 983048 | tf_op jit(solution)/shard_map/ppermute | solution.py:352
  163.6 10.7 %factor_one.1 = (f32[64,512]{1,0:T(8,128)S(1)}, f32[4,512,128]{2,1,0:T(8,128)S(1)}, f32[5,128,128]{2,1,0:T(8,128)S(1)}, f32[5,128,128]{2,1,0:T(8,128)S(1)}) custom-call(f32[5,128,128]{2,1,0:T(8,128)S(1)} %bitcast.20, f32[5,128,128]{2,1,0:T(8,128)S(1)} %collective-permute-done.1.other_ref, f32[3,64,512]{2,1,0:T(8,128)S(1)} %bitcast.16, s32[3]{0:T(128)S(1)} %copy-done.1, ...), custom_call_target="tpu_custom_call" | custom-call | tf_op jit(solution)/shard_map/factor_one/pallas_call | solution.py:207
  174.7 1.3 collective-permute-done.2
  176.0 11.4 %all_to_all.64 = f32[16,40,128]{2,1,0:T(8,128)S(1)} all-to-all(f32[16,40,128]{2,1,0:T(8,128)S(1)} %bitcast.28), channel_id=1, replica_groups=mesh['y'=4,'core'=2,'gy'=4,'gz'=8] {'y','gy'}, dimensions={0} | all-to-all | bytes 655360 | tf_op jit(solution)/shard_map/all_to_all | solution.py:344
  187.5 10.8 %all_to_all.65 = f32[8,40,128]{2,1,0:T(8,128)S(1)} all-to-all(f32[8,40,128]{2,1,0:T(8,128)S(1)} %broadcast_in_dim.14), channel_id=1, replica_groups=mesh['y'=4,'core'=2,'gy'=4,'gz'=8] {'gz'}, dimensions={0} | all-to-all | bytes 327680 | tf_op jit(solution)/shard_map/all_to_all | solution.py:344
  198.3 10.5 %all_to_all.66 = f32[16,40,128]{2,1,0:T(8,128)S(1)} all-to-all(f32[16,40,128]{2,1,0:T(8,128)S(1)} %broadcast_in_dim.15), channel_id=1, replica_groups=mesh['y'=4,'core'=2,'gy'=4,'gz'=8] {'y','gy'}, dimensions={0} | all-to-all | bytes 655360 | tf_op jit(solution)/shard_map/all_to_all | solution.py:344
  208.9 3.9 %collective-permute-start.3 = (f32[5,128,128]{2,1,0:T(8,128)S(1)}, f32[5,128,128]{2,1,0:T(8,128)S(1)}, u32[]{:S(2)}, u32[]{:S(2)}) collective-permute-start(f32[5,128,128]{2,1,0:T(8,128)S(1)} %bitcast.23), channel_id=1, source_target_pairs={{0,32},{32,0},{1,33},{33,1},{2,34},{34,2},{3,35},{35,3},{4,36},{36... | collective-permute-start | bytes 983048 | tf_op jit(solution)/shard_map/ppermute | solution.py:352
  214.0 9.3 %factor_two.1 = (f32[64,512]{1,0:T(8,128)S(1)}, f32[32,8,128]{2,1,0:T(8,128)S(1)}) custom-call(f32[5,128,128]{2,1,0:T(8,128)S(1)} %bitcast.24, f32[5,128,128]{2,1,0:T(8,128)S(1)} %collective-permute-done.3.other_ref, f32[3,64,512]{2,1,0:T(8,128)S(1)} %bitcast.17, s32[3]{0:T(128)S(1)} %copy-done.1, s32[1]{0:T(128)} %bitcast.place_ref, ...), custom_call_target="tpu_custom_call" | custom-call | tf_op jit(solution)/shard_map/factor_two/pallas_call | solution.py:248
  223.3 11.4 %all_to_all.67.y_ref = f32[32,8,128]{2,1,0:T(8,128)} all-to-all(f32[32,8,128]{2,1,0:T(8,128)S(1)} %get-tuple-element.26), channel_id=1, replica_groups=mesh['y'=4,'core'=2,'gy'=4,'gz'=8] {'y','core','gy'}, dimensions={0} | all-to-all | bytes 262144 | tf_op jit(solution)/shard_map/all_to_all | solution.py:344
  234.8 1.9 pack.1
  236.6 11.8 %all_to_all.68.y_ref = f32[8,32,128]{2,1,0:T(8,128)S(1)} all-to-all(f32[8,32,128]{2,1,0:T(8,128)} %pack.1), channel_id=1, replica_groups=mesh['y'=4,'core'=2,'gy'=4,'gz'=8] {'gz'}, dimensions={0} | all-to-all | bytes 262144 | tf_op jit(solution)/shard_map/all_to_all | solution.py:344
  249.0 1.6 collective-permute-start.4
  251.9 11.5 %all_to_all.69 = f32[16,40,128]{2,1,0:T(8,128)S(1)} all-to-all(f32[16,40,128]{2,1,0:T(8,128)S(1)} %bitcast.29), channel_id=1, replica_groups=mesh['y'=4,'core'=2,'gy'=4,'gz'=8] {'y','gy'}, dimensions={0} | all-to-all | bytes 655360 | tf_op jit(solution)/shard_map/all_to_all | solution.py:344
  263.4 10.7 %all_to_all.70 = f32[8,40,128]{2,1,0:T(8,128)S(1)} all-to-all(f32[8,40,128]{2,1,0:T(8,128)S(1)} %broadcast_in_dim.16), channel_id=1, replica_groups=mesh['y'=4,'core'=2,'gy'=4,'gz'=8] {'gz'}, dimensions={0} | all-to-all | bytes 327680 | tf_op jit(solution)/shard_map/all_to_all | solution.py:344
  274.2 10.6 %all_to_all.71 = f32[16,40,128]{2,1,0:T(8,128)S(1)} all-to-all(f32[16,40,128]{2,1,0:T(8,128)S(1)} %broadcast_in_dim.17), channel_id=1, replica_groups=mesh['y'=4,'core'=2,'gy'=4,'gz'=8] {'y','gy'}, dimensions={0} | all-to-all | bytes 655360 | tf_op jit(solution)/shard_map/all_to_all | solution.py:344
  284.8 3.9 %collective-permute-start.5 = (f32[5,128,128]{2,1,0:T(8,128)S(1)}, f32[5,128,128]{2,1,0:T(8,128)S(1)}, u32[]{:S(2)}, u32[]{:S(2)}) collective-permute-start(f32[5,128,128]{2,1,0:T(8,128)S(1)} %bitcast.21), channel_id=1, source_target_pairs={{0,32},{32,0},{1,33},{33,1},{2,34},{34,2},{3,35},{35,3},{4,36},{36... | collective-permute-start | bytes 983048 | tf_op jit(solution)/shard_map/ppermute | solution.py:352
  289.9 9.1 %factor_three.1 = (f32[3,64,512]{2,1,0:T(8,128)}, f32[4,2,8,64]{3,2,1,0:T(8,128)}) custom-call(f32[5,128,128]{2,1,0:T(8,128)S(1)} %bitcast.22, f32[5,128,128]{2,1,0:T(8,128)S(1)} %collective-permute-done.5.other_ref, f32[3,64,512]{2,1,0:T(8,128)S(1)} %bitcast.18, s32[3]{0:T(128)S(1)} %copy-done.1, s32[1]{0:T(128)} %bitcast.place_ref, ...), custom_call_target="tpu_custom_call" | custom-call | tf_op jit(solution)/shard_map/factor_three/pallas_call | solution.py:326
  (26 shorter events, 7.7 us)
Async XLA Ops:
  108.1 55.4 %copy-start = (f32[3,512,64]{1,2,0:T(8,128)S(1)}, f32[3,512,64]{1,2,0:T(8,128)}, u32[]{:S(2)}) copy-start(f32[3,512,64]{1,2,0:T(8,128)} %param.4) | copy-start | bytes 1179652
  108.1 55.4 %copy-start.1 = (s32[3]{0:T(128)S(1)}, s32[3]{0:T(128)}, u32[]{:S(2)}) copy-start(s32[3]{0:T(128)} %rank_ref.5) | copy-start | bytes 40
  116.2 2.5 collective-permute-start
  158.4 5.2 %collective-permute-start.1 = (f32[5,128,128]{2,1,0:T(8,128)S(1)}, f32[5,128,128]{2,1,0:T(8,128)S(1)}, u32[]{:S(2)}, u32[]{:S(2)}) collective-permute-start(f32[5,128,128]{2,1,0:T(8,128)S(1)} %bitcast.19), channel_id=1, source_target_pairs={{0,32},{32,0},{1,33},{33,1},{2,34},{34,2},{3,35},{35,3},{4,36},{36... | collective-permute-start | bytes 983048 | tf_op jit(solution)/shard_map/ppermute | solution.py:352
  174.3 1.7 collective-permute-start.2
  208.9 5.2 %collective-permute-start.3 = (f32[5,128,128]{2,1,0:T(8,128)S(1)}, f32[5,128,128]{2,1,0:T(8,128)S(1)}, u32[]{:S(2)}, u32[]{:S(2)}) collective-permute-start(f32[5,128,128]{2,1,0:T(8,128)S(1)} %bitcast.23), channel_id=1, source_target_pairs={{0,32},{32,0},{1,33},{33,1},{2,34},{34,2},{3,35},{35,3},{4,36},{36... | collective-permute-start | bytes 983048 | tf_op jit(solution)/shard_map/ppermute | solution.py:352
  249.0 2.9 collective-permute-start.4
  284.8 5.2 %collective-permute-start.5 = (f32[5,128,128]{2,1,0:T(8,128)S(1)}, f32[5,128,128]{2,1,0:T(8,128)S(1)}, u32[]{:S(2)}, u32[]{:S(2)}) collective-permute-start(f32[5,128,128]{2,1,0:T(8,128)S(1)} %bitcast.21), channel_id=1, source_target_pairs={{0,32},{32,0},{1,33},{33,1},{2,34},{34,2},{3,35},{35,3},{4,36},{36... | collective-permute-start | bytes 983048 | tf_op jit(solution)/shard_map/ppermute | solution.py:352

commit v4 on v3

--- a/solution.py
+++ b/solution.py
@@ -225,23 +225,28 @@
     )(*halves, starts, ranks, place, x2)
 
 
-def factor_two_kernel(mine_ref, other_ref, start_ref, rank_ref, place_ref, a_ref, u_ref, y_ref, gh_ref, gl_ref):
+def factor_two_kernel(
+    mine_ref, other_ref, start_ref, rank_ref, place_ref, a_ref, u_ref, out_ref, gh_ref, gl_ref, y_ref
+):
     v = masked_factor((mine_ref, other_ref), start_ref, rank_ref, place_ref, 1, gh_ref, gl_ref)
     u_ref[...] = v
     vh, vl = split(v)
     vs = jnp.concatenate([vh, vl], axis=0)
     ah, al = split(jnp.concatenate([a_ref[q] for q in range(4)], axis=1))
     y = mm(ah, vs, NT) + mm(al, vs, NT)
-    y = y + pltpu.roll(y, R, 1)
-    rolled = [y if k == 0 else pltpu.roll(y, 8 * k, 1) for k in range(8)]
+    y_ref[...] = y + pltpu.roll(y, R, 1)
     group = lax.broadcasted_iota(jnp.int32, (8, 128), 1) // 8
-    for bx in range(8):
-        for by in range(4):
-            tile = jnp.zeros((8, 128), F32)
-            for r in range(16):
-                at = (by * 16 + r) * 8
-                tile = jnp.where(group == r, rolled[(r - bx) % 8][at : at + 8, :], tile)
-            y_ref[bx * 4 + by] = tile
+    for by in range(4):
+        tiles = [jnp.zeros((8, 128), F32) for _ in range(8)]
+        for p in range(8):
+            for e in range(2):
+                rows = y_ref[pl.ds(by * 128 + e * 8 + p, 8, stride=16), :]
+                for bx in range(8):
+                    shift = (2 * p + e - bx) % 8
+                    moved = pltpu.roll(rows, 8 * shift, 1) if shift else rows
+                    tiles[bx] = jnp.where(group == 2 * p + e, moved, tiles[bx])
+        for bx in range(8):
+            out_ref[bx * 32 + by * 8 : bx * 32 + by * 8 + 8, :] = tiles[bx]
 
 
 def factor_two(halves, starts, ranks, place, a):
@@ -249,45 +254,28 @@
         factor_two_kernel,
         out_shape=(
             jax.ShapeDtypeStruct((R, N), F32),
-            jax.ShapeDtypeStruct((32, 8, 128), F32),
+            jax.ShapeDtypeStruct((256, 128), F32),
         ),
         in_specs=[VMEM, VMEM, VMEM, SMEM, SMEM, VMEM],
         out_specs=(VMEM, VMEM),
-        scratch_shapes=[pltpu.VMEM((N, N), BF), pltpu.VMEM((N, N), BF)],
+        scratch_shapes=[pltpu.VMEM((N, N), BF), pltpu.VMEM((N, N), BF), pltpu.VMEM((N, 128), F32)],
         compiler_params=pltpu.CompilerParams(vmem_limit_bytes=32 * 2**20),
         name="factor_two",
     )(*halves, starts, ranks, place, a)
 
 
-def pack_kernel(y_ref, out_ref):
-    group = lax.broadcasted_iota(jnp.int32, (32, 128), 1) // 16
-    for z in range(8):
-        rows = jnp.zeros((32, 128), F32)
-        for g in range(8):
-            at = 8 * (g % 4) + 4 * (g // 4)
-            tile = y_ref[at : at + 4].reshape(32, 128)
-            if g != z:
-                tile = pltpu.roll(tile, (16 * (g - z)) % 128, 1)
-            rows = jnp.where(group == g, tile, rows)
-        out_ref[z] = rows
-
-
-def pack(y):
-    return pl.pallas_call(
-        pack_kernel,
-        out_shape=jax.ShapeDtypeStruct((8, 32, 128), F32),
-        in_specs=[VMEM],
-        out_specs=VMEM,
-        name="pack",
-    )(y)
-
-
 def gram_three_kernel(place_ref, y_ref, keep_ref, send_ref, b_ref):
-    lane = lax.broadcasted_iota(jnp.int32, (32, 128), 1)
-    for z in range(8):
-        y = y_ref[z]
-        b_ref[64 * z : 64 * z + 32, :] = jnp.where(lane < R, y, 0.0)
-        b_ref[64 * z + 32 : 64 * z + 64, :] = jnp.where(lane < R, pltpu.roll(y, R, 1), 0.0)
+    group = lax.broadcasted_iota(jnp.int32, (8, 128), 1) // 16
+    for pg in range(8):
+        for p in range(8):
+            rows = jnp.zeros((8, 128), F32)
+            for s in range(4):
+                at = (8 * s + pg) * 8
+                tile = y_ref[at : at + 8, :]
+                if s != p:
+                    tile = pltpu.roll(tile, (16 * (s - p)) % 128, 1)
+                rows = jnp.where(group == s, tile, rows)
+            b_ref[pl.ds(8 * pg + p, 8, stride=R), :] = rows
     bh, bl = split(b_ref[...])
     low = mm(bh[:256], bh, NT) + mm(bh[:256], bl, NT) + mm(bl[:256], bh, NT)
     high = mm(bh[256:], bh[256:], NT) + mm(bh[256:], bl[256:], NT) + mm(bl[256:], bh[256:], NT)
@@ -369,8 +357,8 @@
     keep, send, x2 = gram_one(place, x)
     u_one, a, keep, send = factor_one(total(keep, send), starts_t, trunc_ranks, place, x2)
     u_two, y = factor_two(total(keep, send), starts_t, trunc_ranks, place, a)
-    y = pack(swap(y, ("y", "core", "gy")))
-    keep, send, b = gram_three(place, swap(y, "gz"))
+    y = swap(y.reshape(256, 1, 128), ("y", "core", "gy", "gz")).reshape(256, 128)
+    keep, send, b = gram_three(place, y)
     factors, core_out = factor_three(total(keep, send), starts_t, trunc_ranks, place, b, u_one, u_two)
     return (jnp.swapaxes(core_out, 2, 3), jnp.swapaxes(factors, 1, 2))
 

time: 300 us -> 292 us (0.973)
  blocking collectives: 231 us -> 227 us
    all_to_all x12 -> x11, blocking collectives: 231 us -> 227 us  [swap(): return lax.all_to_all(x, axes, 0, 0, tiled=True)]
where the time goes in v4:
time: 292 us
  blocking collectives  227 us (78%)
  Pallas kernels  38.1 us (13%)
  starting transfers between devices  14 us (5%)
  waiting for transfers between devices  7.54 us (3%)
  local copies, waits for them, and re-layouts  4.55 us (2%)
    all_to_all x11, blocking collectives, swap(): return lax.all_to_all(x, axes, 0, 0, tiled=True)  227 us
    ppermute x6, starting transfers between devices, other_core(): return lax.ppermute(x, 'core', [(0, 1), (1, 0)])  14 us
    pallas_call x1, Pallas kernels, factor_one(): pl.pallas_call(factor_one_kernel, out_shape=(jax.ShapeDtypeStruct((R, N),...  10.7 us
    pallas_call x1, Pallas kernels, factor_two(): pl.pallas_call(factor_two_kernel, out_shape=(jax.ShapeDtypeStruct((R, N),...  9.3 us
    pallas_call x1, Pallas kernels, factor_three(): pl.pallas_call(factor_three_kernel, out_shape=(jax.ShapeDtypeStruct((3, R...  9.1 us
    pallas_call x1, Pallas kernels, gram_one(): pl.pallas_call(gram_one_kernel, grid=(4,), out_shape=(HALF, HALF, pltpu.H...  8.1 us
    ppermute x6, waiting for transfers between devices, other_core(): return lax.ppermute(x, 'core', [(0, 1), (1, 0)])  7.54 us
  transfers between devices with their start and end apart: 6, of which 6 were waited for; matrix products, arithmetic and copies ran while one was open for 0% of the time, Pallas kernels for 0%

profile of v4, /device:TPU:1, one launch (start us, length us, event | category | flops | bytes accessed | tf_op | source)
XLA Modules:
  0.0 291.9 jit_solution(14241379005895120119)
XLA Ops:
  0.6 4.4 %copy.8 = f32[4,8,64,8,128]{4,3,2,1,0:T(8,128)S(1)} copy(f32[4,8,64,8,128]{4,3,1,2,0:T(8,128)} %bitcast.32) | data formatting | bytes 16777216 | tf_op jit(solution)/shard_map/transpose | solution.py:355
  5.1 103.1 %all_to_all.55 = f32[32,512,128]{2,1,0:T(8,128)S(1)} all-to-all(f32[32,512,128]{2,1,0:T(8,128)S(1)} %bitcast.31), channel_id=1, replica_groups=mesh['y'=4,'core'=2,'gy'=4,'gz'=8] {'y','core','gy'}, dimensions={0} | all-to-all | bytes 16777216 | tf_op jit(solution)/shard_map/all_to_all | solution.py:332
  108.1 8.1 %gram_one.1 = (f32[5,128,128]{2,1,0:T(8,128)S(1)}, f32[5,128,128]{2,1,0:T(8,128)S(1)}, bf16[2,8,512,512]{3,2,1,0:T(8,128)(2,1)}) custom-call(s32[1]{0:T(128)} %bitcast.place_ref, f32[8,4,512,128]{3,2,1,0:T(8,128)S(1)} %bitcast.19), custom_call_target="tpu_custom_call" | custom-call | tf_op jit(solution)/shard_map/gram_one/pallas_call | solution.py:171
  116.2 1.3 collective-permute-start
  118.8 12.3 %all_to_all.56 = f32[16,40,128]{2,1,0:T(8,128)S(1)} all-to-all(f32[16,40,128]{2,1,0:T(8,128)S(1)} %bitcast.33), channel_id=1, replica_groups=mesh['y'=4,'core'=2,'gy'=4,'gz'=8] {'y','gy'}, dimensions={0} | all-to-all | bytes 655360 | tf_op jit(solution)/shard_map/all_to_all | solution.py:332
  131.1 16.3 %all_to_all.57 = f32[8,40,128]{2,1,0:T(8,128)S(1)} all-to-all(f32[8,40,128]{2,1,0:T(8,128)S(1)} %broadcast_in_dim.12), channel_id=1, replica_groups=mesh['y'=4,'core'=2,'gy'=4,'gz'=8] {'gz'}, dimensions={0} | all-to-all | bytes 327680 | tf_op jit(solution)/shard_map/all_to_all | solution.py:332
  147.5 10.9 %all_to_all.58 = f32[16,40,128]{2,1,0:T(8,128)S(1)} all-to-all(f32[16,40,128]{2,1,0:T(8,128)S(1)} %broadcast_in_dim.13), channel_id=1, replica_groups=mesh['y'=4,'core'=2,'gy'=4,'gz'=8] {'y','gy'}, dimensions={0} | all-to-all | bytes 655360 | tf_op jit(solution)/shard_map/all_to_all | solution.py:332
  158.4 3.9 %collective-permute-start.1 = (f32[5,128,128]{2,1,0:T(8,128)S(1)}, f32[5,128,128]{2,1,0:T(8,128)S(1)}, u32[]{:S(2)}, u32[]{:S(2)}) collective-permute-start(f32[5,128,128]{2,1,0:T(8,128)S(1)} %bitcast.23), channel_id=1, source_target_pairs={{0,32},{32,0},{1,33},{33,1},{2,34},{34,2},{3,35},{35,3},{4,36},{36... | collective-permute-start | bytes 983048 | tf_op jit(solution)/shard_map/ppermute | solution.py:340
  163.6 10.7 %factor_one.1 = (f32[64,512]{1,0:T(8,128)S(1)}, f32[4,512,128]{2,1,0:T(8,128)S(1)}, f32[5,128,128]{2,1,0:T(8,128)S(1)}, f32[5,128,128]{2,1,0:T(8,128)S(1)}) custom-call(f32[5,128,128]{2,1,0:T(8,128)S(1)} %bitcast.24, f32[5,128,128]{2,1,0:T(8,128)S(1)} %collective-permute-done.1.other_ref, f32[3,64,512]{2,1,0:T(8,128)S(1)} %bitcast.20, s32[3]{0:T(128)S(1)} %copy-done.1, ...), custom_call_target="tpu_custom_call" | custom-call | tf_op jit(solution)/shard_map/factor_one/pallas_call | solution.py:207
  174.7 1.3 collective-permute-done.2
  176.0 11.4 %all_to_all.59 = f32[16,40,128]{2,1,0:T(8,128)S(1)} all-to-all(f32[16,40,128]{2,1,0:T(8,128)S(1)} %bitcast.34), channel_id=1, replica_groups=mesh['y'=4,'core'=2,'gy'=4,'gz'=8] {'y','gy'}, dimensions={0} | all-to-all | bytes 655360 | tf_op jit(solution)/shard_map/all_to_all | solution.py:332
  187.5 10.8 %all_to_all.60 = f32[8,40,128]{2,1,0:T(8,128)S(1)} all-to-all(f32[8,40,128]{2,1,0:T(8,128)S(1)} %broadcast_in_dim.14), channel_id=1, replica_groups=mesh['y'=4,'core'=2,'gy'=4,'gz'=8] {'gz'}, dimensions={0} | all-to-all | bytes 327680 | tf_op jit(solution)/shard_map/all_to_all | solution.py:332
  198.3 10.5 %all_to_all.61 = f32[16,40,128]{2,1,0:T(8,128)S(1)} all-to-all(f32[16,40,128]{2,1,0:T(8,128)S(1)} %broadcast_in_dim.15), channel_id=1, replica_groups=mesh['y'=4,'core'=2,'gy'=4,'gz'=8] {'y','gy'}, dimensions={0} | all-to-all | bytes 655360 | tf_op jit(solution)/shard_map/all_to_all | solution.py:332
  208.9 3.9 %collective-permute-start.3 = (f32[5,128,128]{2,1,0:T(8,128)S(1)}, f32[5,128,128]{2,1,0:T(8,128)S(1)}, u32[]{:S(2)}, u32[]{:S(2)}) collective-permute-start(f32[5,128,128]{2,1,0:T(8,128)S(1)} %bitcast.27), channel_id=1, source_target_pairs={{0,32},{32,0},{1,33},{33,1},{2,34},{34,2},{3,35},{35,3},{4,36},{36... | collective-permute-start | bytes 983048 | tf_op jit(solution)/shard_map/ppermute | solution.py:340
  212.8 1.3 collective-permute-done.3.other_ref
  214.0 9.3 %factor_two.1 = (f32[64,512]{1,0:T(8,128)S(1)}, f32[256,128]{1,0:T(8,128)S(1)}) custom-call(f32[5,128,128]{2,1,0:T(8,128)S(1)} %bitcast.28, f32[5,128,128]{2,1,0:T(8,128)S(1)} %collective-permute-done.3.other_ref, f32[3,64,512]{2,1,0:T(8,128)S(1)} %bitcast.21, s32[3]{0:T(128)S(1)} %copy-done.1, s32[1]{0:T(128)} %bitcast.place_ref, ...), custom_call_target="tpu_custom_call" | custom-call | tf_op jit(solution)/shard_map/factor_two/pallas_call | solution.py:253
  223.4 18.3 %all_to_all.62 = f32[256,1,128]{2,1,0:T(1,128)S(1)} all-to-all(f32[256,1,128]{2,1,0:T(1,128)S(1)} %bitcast.30), channel_id=1, replica_groups=mesh['y'=4,'core'=2,'gy'=4,'gz'=8] {'y','core','gy','gz'}, dimensions={0} | all-to-all | bytes 262144 | tf_op jit(solution)/shard_map/all_to_all | solution.py:332
  243.1 1.3 collective-permute-done.4
  244.4 11.7 %all_to_all.63 = f32[16,40,128]{2,1,0:T(8,128)S(1)} all-to-all(f32[16,40,128]{2,1,0:T(8,128)S(1)} %bitcast.35), channel_id=1, replica_groups=mesh['y'=4,'core'=2,'gy'=4,'gz'=8] {'y','gy'}, dimensions={0} | all-to-all | bytes 655360 | tf_op jit(solution)/shard_map/all_to_all | solution.py:332
  256.2 10.8 %all_to_all.64 = f32[8,40,128]{2,1,0:T(8,128)S(1)} all-to-all(f32[8,40,128]{2,1,0:T(8,128)S(1)} %broadcast_in_dim.16), channel_id=1, replica_groups=mesh['y'=4,'core'=2,'gy'=4,'gz'=8] {'gz'}, dimensions={0} | all-to-all | bytes 327680 | tf_op jit(solution)/shard_map/all_to_all | solution.py:332
  267.0 10.6 %all_to_all.65 = f32[16,40,128]{2,1,0:T(8,128)S(1)} all-to-all(f32[16,40,128]{2,1,0:T(8,128)S(1)} %broadcast_in_dim.17), channel_id=1, replica_groups=mesh['y'=4,'core'=2,'gy'=4,'gz'=8] {'y','gy'}, dimensions={0} | all-to-all | bytes 655360 | tf_op jit(solution)/shard_map/all_to_all | solution.py:332
  277.6 3.9 %collective-permute-start.5 = (f32[5,128,128]{2,1,0:T(8,128)S(1)}, f32[5,128,128]{2,1,0:T(8,128)S(1)}, u32[]{:S(2)}, u32[]{:S(2)}) collective-permute-start(f32[5,128,128]{2,1,0:T(8,128)S(1)} %bitcast.25), channel_id=1, source_target_pairs={{0,32},{32,0},{1,33},{33,1},{2,34},{34,2},{3,35},{35,3},{4,36},{36... | collective-permute-start | bytes 983048 | tf_op jit(solution)/shard_map/ppermute | solution.py:340
  281.5 1.3 collective-permute-done.5.other_ref
  282.8 9.1 %factor_three.1 = (f32[3,64,512]{2,1,0:T(8,128)}, f32[4,2,8,64]{3,2,1,0:T(8,128)}) custom-call(f32[5,128,128]{2,1,0:T(8,128)S(1)} %bitcast.26, f32[5,128,128]{2,1,0:T(8,128)S(1)} %collective-permute-done.5.other_ref, f32[3,64,512]{2,1,0:T(8,128)S(1)} %bitcast.22, s32[3]{0:T(128)S(1)} %copy-done.1, s32[1]{0:T(128)} %bitcast.place_ref, ...), custom_call_target="tpu_custom_call" | custom-call | tf_op jit(solution)/shard_map/factor_three/pallas_call | solution.py:314
  (24 shorter events, 4.8 us)
Async XLA Ops:
  108.1 55.4 %copy-start = (f32[3,512,64]{1,2,0:T(8,128)S(1)}, f32[3,512,64]{1,2,0:T(8,128)}, u32[]{:S(2)}) copy-start(f32[3,512,64]{1,2,0:T(8,128)} %param.4) | copy-start | bytes 1179652
  108.1 55.4 %copy-start.1 = (s32[3]{0:T(128)S(1)}, s32[3]{0:T(128)}, u32[]{:S(2)}) copy-start(s32[3]{0:T(128)} %rank_ref.5) | copy-start | bytes 40
  116.2 2.5 collective-permute-start
  158.4 5.2 %collective-permute-start.1 = (f32[5,128,128]{2,1,0:T(8,128)S(1)}, f32[5,128,128]{2,1,0:T(8,128)S(1)}, u32[]{:S(2)}, u32[]{:S(2)}) collective-permute-start(f32[5,128,128]{2,1,0:T(8,128)S(1)} %bitcast.23), channel_id=1, source_target_pairs={{0,32},{32,0},{1,33},{33,1},{2,34},{34,2},{3,35},{35,3},{4,36},{36... | collective-permute-start | bytes 983048 | tf_op jit(solution)/shard_map/ppermute | solution.py:340
  174.3 1.7 collective-permute-start.2
  208.9 5.2 %collective-permute-start.3 = (f32[5,128,128]{2,1,0:T(8,128)S(1)}, f32[5,128,128]{2,1,0:T(8,128)S(1)}, u32[]{:S(2)}, u32[]{:S(2)}) collective-permute-start(f32[5,128,128]{2,1,0:T(8,128)S(1)} %bitcast.27), channel_id=1, source_target_pairs={{0,32},{32,0},{1,33},{33,1},{2,34},{34,2},{3,35},{35,3},{4,36},{36... | collective-permute-start | bytes 983048 | tf_op jit(solution)/shard_map/ppermute | solution.py:340
  242.5 1.9 collective-permute-start.4
  277.6 5.2 %collective-permute-start.5 = (f32[5,128,128]{2,1,0:T(8,128)S(1)}, f32[5,128,128]{2,1,0:T(8,128)S(1)}, u32[]{:S(2)}, u32[]{:S(2)}) collective-permute-start(f32[5,128,128]{2,1,0:T(8,128)S(1)} %bitcast.25), channel_id=1, source_target_pairs={{0,32},{32,0},{1,33},{33,1},{2,34},{34,2},{3,35},{35,3},{4,36},{36... | collective-permute-start | bytes 983048 | tf_op jit(solution)/shard_map/ppermute | solution.py:340

commit v5 on v4

--- a/solution.py
+++ b/solution.py
@@ -67,19 +67,21 @@
         for k in range(8):
             pivot = row(diag[k], k)
             inv = 1.0 / pivot
-            scaled_row = row(m[b0], k) * inv
-            rest = jnp.where(row8 > k, diag[k], 0.0)
+            rest = jnp.where(row8 > k, diag[k], 0.0) * inv
             pivots = jnp.where(row8 == k, pivot, pivots)
-            factors = {k2: row(diag[k2], k) * inv for k2 in range(k + 1, 8)}
-            for k2 in factors:
-                diag[k2] = diag[k2] - rest * factors[k2]
-            m[b0] = m[b0] - rest * scaled_row
+            pivot_row = row(m[b0], k)
+            heads = {k2: row(diag[k2], k) for k2 in range(k + 1, 8)}
+            for k2 in heads:
+                diag[k2] = diag[k2] - rest * heads[k2]
+            m[b0] = m[b0] - rest * pivot_row
             for n in range(7 - b0):
-                m[b0 + 1 + n] = m[b0 + 1 + n] - below[k][n] * scaled_row
-                for k2 in factors:
-                    below[k2][n] = below[k2][n] - below[k][n] * factors[k2]
-            for k2 in range(len(ahead)):
-                ahead[k2] = ahead[k2] - below[k][0] * (row(below[k][0], k2) * inv)
+                ratio = below[k][n] * inv
+                m[b0 + 1 + n] = m[b0 + 1 + n] - ratio * pivot_row
+                for k2 in heads:
+                    below[k2][n] = below[k2][n] - ratio * heads[k2]
+                if n == 0:
+                    for k2 in range(8):
+                        ahead[k2] = ahead[k2] - below[k][0] * row(ratio, k2)
         scale.append(pivots)
         diag = ahead
     out = []
@@ -136,6 +138,30 @@
     return jnp.where(index < rank_ref[mode], v, 0.0)
 
 
+def regroup_kernel(x_hbm, out_ref, sem):
+    copies = [
+        pltpu.make_async_copy(x_hbm.at[s, :, pl.ds(8 * g, 8), :], out_ref.at[8 * s + g], sem.at[8 * s + g])
+        for s in range(4)
+        for g in range(8)
+    ]
+    for c in copies:
+        c.start()
+    for c in copies:
+        c.wait()
+
+
+def regroup(x):
+    return pl.pallas_call(
+        regroup_kernel,
+        out_shape=jax.ShapeDtypeStruct((32, 64, 8, 128), F32),
+        in_specs=[HBM],
+        out_specs=VMEM,
+        scratch_shapes=[pltpu.SemaphoreType.DMA((32,))],
+        compiler_params=pltpu.CompilerParams(vmem_limit_bytes=42 * 2**20),
+        name="regroup",
+    )(x)
+
+
 def gram_one_kernel(place_ref, x_ref, keep_ref, send_ref, x2_ref, low_ref, high_ref, cross_ref):
     step = pl.program_id(0)
 
@@ -145,17 +171,20 @@
         high_ref[...] = jnp.zeros_like(high_ref)
         cross_ref[...] = jnp.zeros_like(cross_ref)
 
-    for p in range(8):
-        for g in range(8):
-            hi, lo = split(x_ref[g, 0, pl.ds(p, 64, stride=8), :])
-            x2_ref[0, p, g * 64 : g * 64 + 64, :] = hi
-            x2_ref[1, p, g * 64 : g * 64 + 64, :] = lo
-    for p in range(0, 8, 4):
-        xh = jnp.concatenate([x2_ref[0, p + k] for k in range(4)], axis=1)
-        xl = jnp.concatenate([x2_ref[1, p + k] for k in range(4)], axis=1)
+    for p in range(0, 8, 2):
+        his, los = [], []
+        for k in (p, p + 1):
+            parts = [split(x_ref[g, 0, pl.ds(k, 64, stride=8), :]) for g in range(8)]
+            hi = jnp.concatenate([h for h, _ in parts], axis=0)
+            lo = jnp.concatenate([l for _, l in parts], axis=0)
+            x2_ref[0, k] = hi
+            x2_ref[1, k] = lo
+            his.append(hi)
+            los.append(lo)
+        xh = jnp.concatenate(his, axis=1)
         low_ref[...] += mm(xh[:256], xh, NT)
         high_ref[...] += mm(xh[256:], xh[256:], NT)
-        cross_ref[...] += mm(xh, xl, NT)
+        cross_ref[...] += mm(xh, jnp.concatenate(los, axis=1), NT)
 
     @pl.when(step == pl.num_programs(0) - 1)
     def _():
@@ -352,7 +381,7 @@
     starts_t = jnp.swapaxes(starts, 1, 2)
     place = lax.axis_index("core").astype(jnp.int32).reshape(1)
     tensor, place = lax.optimization_barrier((tensor, place))
-    x = tensor.reshape(4, 64, 8, 8, 128).transpose(0, 2, 1, 3, 4).reshape(32, N, 128)
+    x = regroup(tensor).reshape(32, N, 128)
     x = swap(x, ("y", "core", "gy")).reshape(8, 4, N, 128)
     keep, send, x2 = gram_one(place, x)
     u_one, a, keep, send = factor_one(total(keep, send), starts_t, trunc_ranks, place, x2)

time: 292 us -> 288 us (0.986)
  local copies, waits for them, and re-layouts: 4.55 us -> 0.12 us
    transpose x1 -> x0, local copies, waits for them, and re-layouts: 4.44 us -> none  [local(): tensor.reshape(4, 64, 8, 8, 128).transpose(0, 2, 1, 3, 4)]
    pallas_call x0 -> x1, Pallas kernels: none -> 3.77 us  [regroup(): pl.pallas_call(regroup_kernel, out_shape=jax.ShapeDtypeStruct((32, 64, 8,...]
where the time goes in v5:
time: 288 us
  blocking collectives  227 us (79%)
  Pallas kernels  38.6 us (13%)
  starting transfers between devices  14.1 us (5%)
  waiting for transfers between devices  7.54 us (3%)
    all_to_all x11, blocking collectives, swap(): return lax.all_to_all(x, axes, 0, 0, tiled=True)  227 us
    ppermute x6, starting transfers between devices, other_core(): return lax.ppermute(x, 'core', [(0, 1), (1, 0)])  14.1 us
    pallas_call x1, Pallas kernels, factor_one(): pl.pallas_call(factor_one_kernel, out_shape=(jax.ShapeDtypeStruct((R, N),...  9.85 us
    pallas_call x1, Pallas kernels, factor_two(): pl.pallas_call(factor_two_kernel, out_shape=(jax.ShapeDtypeStruct((R, N),...  8.46 us
    pallas_call x1, Pallas kernels, factor_three(): pl.pallas_call(factor_three_kernel, out_shape=(jax.ShapeDtypeStruct((3, R...  8.26 us
    ppermute x6, waiting for transfers between devices, other_core(): return lax.ppermute(x, 'core', [(0, 1), (1, 0)])  7.54 us
    pallas_call x1, Pallas kernels, gram_one(): pl.pallas_call(gram_one_kernel, grid=(4,), out_shape=(HALF, HALF, pltpu.H...  7.38 us
  transfers between devices with their start and end apart: 6, of which 6 were waited for; matrix products, arithmetic and copies ran while one was open for 0% of the time, Pallas kernels for 0%

profile of v5, /device:TPU:1, one launch (start us, length us, event | category | flops | bytes accessed | tf_op | source)
XLA Modules:
  0.0 287.9 jit_solution(14522277817441985894)
XLA Ops:
  0.6 3.8 %regroup.1 = f32[32,64,8,128]{3,2,1,0:T(8,128)S(1)} custom-call(f32[4,64,64,128]{3,2,1,0:T(8,128)} %x_hbm), custom_call_target="tpu_custom_call" | custom-call | tf_op jit(solution)/shard_map/regroup/pallas_call | solution.py:154
  4.4 103.1 %all_to_all.55 = f32[32,512,128]{2,1,0:T(8,128)S(1)} all-to-all(f32[32,512,128]{2,1,0:T(8,128)S(1)} %bitcast.17), channel_id=1, replica_groups=mesh['y'=4,'core'=2,'gy'=4,'gz'=8] {'y','core','gy'}, dimensions={0} | all-to-all | bytes 16777216 | tf_op jit(solution)/shard_map/all_to_all | solution.py:361
  107.5 7.4 %gram_one.1 = (f32[5,128,128]{2,1,0:T(8,128)S(1)}, f32[5,128,128]{2,1,0:T(8,128)S(1)}, bf16[2,8,512,512]{3,2,1,0:T(8,128)(2,1)}) custom-call(s32[1]{0:T(128)} %bitcast.place_ref, f32[8,4,512,128]{3,2,1,0:T(8,128)S(1)} %bitcast.16), custom_call_target="tpu_custom_call" | custom-call | tf_op jit(solution)/shard_map/gram_one/pallas_call | solution.py:200
  114.9 1.3 collective-permute-start
  116.1 1.3 collective-permute-done
  117.4 12.3 %all_to_all.56 = f32[16,40,128]{2,1,0:T(8,128)S(1)} all-to-all(f32[16,40,128]{2,1,0:T(8,128)S(1)} %bitcast.29), channel_id=1, replica_groups=mesh['y'=4,'core'=2,'gy'=4,'gz'=8] {'y','gy'}, dimensions={0} | all-to-all | bytes 655360 | tf_op jit(solution)/shard_map/all_to_all | solution.py:361
  129.7 16.3 %all_to_all.57 = f32[8,40,128]{2,1,0:T(8,128)S(1)} all-to-all(f32[8,40,128]{2,1,0:T(8,128)S(1)} %broadcast_in_dim.12), channel_id=1, replica_groups=mesh['y'=4,'core'=2,'gy'=4,'gz'=8] {'gz'}, dimensions={0} | all-to-all | bytes 327680 | tf_op jit(solution)/shard_map/all_to_all | solution.py:361
  146.1 10.9 %all_to_all.58 = f32[16,40,128]{2,1,0:T(8,128)S(1)} all-to-all(f32[16,40,128]{2,1,0:T(8,128)S(1)} %broadcast_in_dim.13), channel_id=1, replica_groups=mesh['y'=4,'core'=2,'gy'=4,'gz'=8] {'y','gy'}, dimensions={0} | all-to-all | bytes 655360 | tf_op jit(solution)/shard_map/all_to_all | solution.py:361
  157.0 3.9 %collective-permute-start.1 = (f32[5,128,128]{2,1,0:T(8,128)S(1)}, f32[5,128,128]{2,1,0:T(8,128)S(1)}, u32[]{:S(2)}, u32[]{:S(2)}) collective-permute-start(f32[5,128,128]{2,1,0:T(8,128)S(1)} %bitcast.21), channel_id=1, source_target_pairs={{0,32},{32,0},{1,33},{33,1},{2,34},{34,2},{3,35},{35,3},{4,36},{36... | collective-permute-start | bytes 983048 | tf_op jit(solution)/shard_map/ppermute | solution.py:369
  160.9 1.3 collective-permute-done.1.other_ref
  162.2 9.8 %factor_one.1 = (f32[64,512]{1,0:T(8,128)S(1)}, f32[4,512,128]{2,1,0:T(8,128)S(1)}, f32[5,128,128]{2,1,0:T(8,128)S(1)}, f32[5,128,128]{2,1,0:T(8,128)S(1)}) custom-call(f32[5,128,128]{2,1,0:T(8,128)S(1)} %bitcast.22, f32[5,128,128]{2,1,0:T(8,128)S(1)} %collective-permute-done.1.other_ref, f32[3,64,512]{2,1,0:T(8,128)S(1)} %bitcast.18, s32[3]{0:T(128)S(1)} %copy-done.1, ...), custom_call_target="tpu_custom_call" | custom-call | tf_op jit(solution)/shard_map/factor_one/pallas_call | solution.py:236
  172.5 1.3 collective-permute-done.2
  173.8 11.4 %all_to_all.59 = f32[16,40,128]{2,1,0:T(8,128)S(1)} all-to-all(f32[16,40,128]{2,1,0:T(8,128)S(1)} %bitcast.30), channel_id=1, replica_groups=mesh['y'=4,'core'=2,'gy'=4,'gz'=8] {'y','gy'}, dimensions={0} | all-to-all | bytes 655360 | tf_op jit(solution)/shard_map/all_to_all | solution.py:361
  185.3 10.8 %all_to_all.60 = f32[8,40,128]{2,1,0:T(8,128)S(1)} all-to-all(f32[8,40,128]{2,1,0:T(8,128)S(1)} %broadcast_in_dim.14), channel_id=1, replica_groups=mesh['y'=4,'core'=2,'gy'=4,'gz'=8] {'gz'}, dimensions={0} | all-to-all | bytes 327680 | tf_op jit(solution)/shard_map/all_to_all | solution.py:361
  196.1 10.5 %all_to_all.61 = f32[16,40,128]{2,1,0:T(8,128)S(1)} all-to-all(f32[16,40,128]{2,1,0:T(8,128)S(1)} %broadcast_in_dim.15), channel_id=1, replica_groups=mesh['y'=4,'core'=2,'gy'=4,'gz'=8] {'y','gy'}, dimensions={0} | all-to-all | bytes 655360 | tf_op jit(solution)/shard_map/all_to_all | solution.py:361
  206.6 3.9 %collective-permute-start.3 = (f32[5,128,128]{2,1,0:T(8,128)S(1)}, f32[5,128,128]{2,1,0:T(8,128)S(1)}, u32[]{:S(2)}, u32[]{:S(2)}) collective-permute-start(f32[5,128,128]{2,1,0:T(8,128)S(1)} %bitcast.25), channel_id=1, source_target_pairs={{0,32},{32,0},{1,33},{33,1},{2,34},{34,2},{3,35},{35,3},{4,36},{36... | collective-permute-start | bytes 983048 | tf_op jit(solution)/shard_map/ppermute | solution.py:369
  210.5 1.3 collective-permute-done.3.other_ref
  211.8 8.5 %factor_two.1 = (f32[64,512]{1,0:T(8,128)S(1)}, f32[256,128]{1,0:T(8,128)S(1)}) custom-call(f32[5,128,128]{2,1,0:T(8,128)S(1)} %bitcast.26, f32[5,128,128]{2,1,0:T(8,128)S(1)} %collective-permute-done.3.other_ref, f32[3,64,512]{2,1,0:T(8,128)S(1)} %bitcast.19, s32[3]{0:T(128)S(1)} %copy-done.1, s32[1]{0:T(128)} %bitcast.place_ref, ...), custom_call_target="tpu_custom_call" | custom-call | tf_op jit(solution)/shard_map/factor_two/pallas_call | solution.py:282
  220.3 18.3 %all_to_all.62 = f32[256,1,128]{2,1,0:T(1,128)S(1)} all-to-all(f32[256,1,128]{2,1,0:T(1,128)S(1)} %bitcast.28), channel_id=1, replica_groups=mesh['y'=4,'core'=2,'gy'=4,'gz'=8] {'y','core','gy','gz'}, dimensions={0} | all-to-all | bytes 262144 | tf_op jit(solution)/shard_map/all_to_all | solution.py:361
  241.3 11.7 %all_to_all.63 = f32[16,40,128]{2,1,0:T(8,128)S(1)} all-to-all(f32[16,40,128]{2,1,0:T(8,128)S(1)} %bitcast.31), channel_id=1, replica_groups=mesh['y'=4,'core'=2,'gy'=4,'gz'=8] {'y','gy'}, dimensions={0} | all-to-all | bytes 655360 | tf_op jit(solution)/shard_map/all_to_all | solution.py:361
  253.1 10.8 %all_to_all.64 = f32[8,40,128]{2,1,0:T(8,128)S(1)} all-to-all(f32[8,40,128]{2,1,0:T(8,128)S(1)} %broadcast_in_dim.16), channel_id=1, replica_groups=mesh['y'=4,'core'=2,'gy'=4,'gz'=8] {'gz'}, dimensions={0} | all-to-all | bytes 327680 | tf_op jit(solution)/shard_map/all_to_all | solution.py:361
  263.9 10.6 %all_to_all.65 = f32[16,40,128]{2,1,0:T(8,128)S(1)} all-to-all(f32[16,40,128]{2,1,0:T(8,128)S(1)} %broadcast_in_dim.17), channel_id=1, replica_groups=mesh['y'=4,'core'=2,'gy'=4,'gz'=8] {'y','gy'}, dimensions={0} | all-to-all | bytes 655360 | tf_op jit(solution)/shard_map/all_to_all | solution.py:361
  274.5 3.9 %collective-permute-start.5 = (f32[5,128,128]{2,1,0:T(8,128)S(1)}, f32[5,128,128]{2,1,0:T(8,128)S(1)}, u32[]{:S(2)}, u32[]{:S(2)}) collective-permute-start(f32[5,128,128]{2,1,0:T(8,128)S(1)} %bitcast.23), channel_id=1, source_target_pairs={{0,32},{32,0},{1,33},{33,1},{2,34},{34,2},{3,35},{35,3},{4,36},{36... | collective-permute-start | bytes 983048 | tf_op jit(solution)/shard_map/ppermute | solution.py:369
  279.7 8.3 %factor_three.1 = (f32[3,64,512]{2,1,0:T(8,128)}, f32[4,2,8,64]{3,2,1,0:T(8,128)}) custom-call(f32[5,128,128]{2,1,0:T(8,128)S(1)} %bitcast.24, f32[5,128,128]{2,1,0:T(8,128)S(1)} %collective-permute-done.5.other_ref, f32[3,64,512]{2,1,0:T(8,128)S(1)} %bitcast.20, s32[3]{0:T(128)S(1)} %copy-done.1, s32[1]{0:T(128)} %bitcast.place_ref, ...), custom_call_target="tpu_custom_call" | custom-call | tf_op jit(solution)/shard_map/factor_three/pallas_call | solution.py:343
  (24 shorter events, 4.8 us)
Async XLA Ops:
  107.5 54.7 %copy-start = (f32[3,512,64]{1,2,0:T(8,128)S(1)}, f32[3,512,64]{1,2,0:T(8,128)}, u32[]{:S(2)}) copy-start(f32[3,512,64]{1,2,0:T(8,128)} %param.4) | copy-start | bytes 1179652
  107.5 54.7 %copy-start.1 = (s32[3]{0:T(128)S(1)}, s32[3]{0:T(128)}, u32[]{:S(2)}) copy-start(s32[3]{0:T(128)} %rank_ref.5) | copy-start | bytes 40
  114.9 2.5 collective-permute-start
  157.0 5.2 %collective-permute-start.1 = (f32[5,128,128]{2,1,0:T(8,128)S(1)}, f32[5,128,128]{2,1,0:T(8,128)S(1)}, u32[]{:S(2)}, u32[]{:S(2)}) collective-permute-start(f32[5,128,128]{2,1,0:T(8,128)S(1)} %bitcast.21), channel_id=1, source_target_pairs={{0,32},{32,0},{1,33},{33,1},{2,34},{34,2},{3,35},{35,3},{4,36},{36... | collective-permute-start | bytes 983048 | tf_op jit(solution)/shard_map/ppermute | solution.py:369
  172.0 1.7 collective-permute-start.2
  206.6 5.2 %collective-permute-start.3 = (f32[5,128,128]{2,1,0:T(8,128)S(1)}, f32[5,128,128]{2,1,0:T(8,128)S(1)}, u32[]{:S(2)}, u32[]{:S(2)}) collective-permute-start(f32[5,128,128]{2,1,0:T(8,128)S(1)} %bitcast.25), channel_id=1, source_target_pairs={{0,32},{32,0},{1,33},{33,1},{2,34},{34,2},{3,35},{35,3},{4,36},{36... | collective-permute-start | bytes 983048 | tf_op jit(solution)/shard_map/ppermute | solution.py:369
  239.4 1.9 collective-permute-start.4
  274.5 5.2 %collective-permute-start.5 = (f32[5,128,128]{2,1,0:T(8,128)S(1)}, f32[5,128,128]{2,1,0:T(8,128)S(1)}, u32[]{:S(2)}, u32[]{:S(2)}) collective-permute-start(f32[5,128,128]{2,1,0:T(8,128)S(1)} %bitcast.23), channel_id=1, source_target_pairs={{0,32},{32,0},{1,33},{33,1},{2,34},{34,2},{3,35},{35,3},{4,36},{36... | collective-permute-start | bytes 983048 | tf_op jit(solution)/shard_map/ppermute | solution.py:369

commit v6 on v5

--- a/solution.py
+++ b/solution.py
@@ -21,6 +21,13 @@
 def split(x):
     hi = x.astype(BF)
     return hi, (x - hi.astype(F32)).astype(BF)
+
+
+def split3(x):
+    hi = x.astype(BF)
+    rest = x - hi.astype(F32)
+    mid = rest.astype(BF)
+    return hi, mid, (rest - mid.astype(F32)).astype(BF)
 
 
 def mm(a, b, dims=NN):
@@ -92,48 +99,49 @@
     return jnp.concatenate(out, axis=0)
 
 
-def subspace(halves, core, start, gh_ref, gl_ref):
+def subspace(halves, core, start, g_ref):
     for here in range(2):
 
         @pl.when(core == here)
         def _():
             for n, (a, b) in enumerate(PAIRS):
                 blk = halves[(n // 5 + here) % 2][n % 5]
-                hi, lo = split(blk)
-                gh_ref[a * 128 : a * 128 + 128, b * 128 : b * 128 + 128] = hi
-                gl_ref[a * 128 : a * 128 + 128, b * 128 : b * 128 + 128] = lo
+                for part, value in enumerate(split3(blk)):
+                    g_ref[part, a * 128 : a * 128 + 128, b * 128 : b * 128 + 128] = value
                 if a != b:
-                    hi, lo = split(blk.T)
-                    gh_ref[b * 128 : b * 128 + 128, a * 128 : a * 128 + 128] = hi
-                    gl_ref[b * 128 : b * 128 + 128, a * 128 : a * 128 + 128] = lo
+                    for part, value in enumerate(split3(blk.T)):
+                        g_ref[part, b * 128 : b * 128 + 128, a * 128 : a * 128 + 128] = value
 
     lane = lax.broadcasted_iota(jnp.int32, (R, 128), 1)
 
-    def image(vh, vs):
-        t = mm(vs, gh_ref[...])
-        return t[:R] + t[R:] + mm(vh, gl_ref[...])
+    def image(w0, w1, w2):
+        t = mm(jnp.concatenate([w0, w1, w2], axis=0), g_ref[0])
+        u = mm(jnp.concatenate([w0, w1], axis=0), g_ref[1])
+        small = t[2 * R :] + u[R:] + mm(w0, g_ref[2])
+        return t[:R] + (t[R : 2 * R] + u[:R]) + small
 
     def step(k, w):
-        wh, wl = split(w)
-        ws = jnp.concatenate([wh, wl], axis=0)
+        w0, w1, w2 = split3(w)
+        ws = jnp.concatenate([w0, w1], axis=0)
         c = mm(ws, ws, NT)
         c = c[:R] + c[R:]
-        z = jnp.where(k == ITERS - 1, w, image(wh, ws))
-        zh, zl = split(z)
+        z0, z1, z2 = split3(jnp.where(k == ITERS - 1, w, image(w0, w1, w2)))
         li = inverse_factor(c + pltpu.roll(c, R, 1))
-        lh = li.astype(BF).astype(F32)
-        both = jnp.where(lane < R, lh, pltpu.roll(li - lh, R, 1)).astype(BF)
+        l0 = li.astype(BF).astype(F32)
+        rest = li - l0
+        l1 = rest.astype(BF).astype(F32)
+        x = jnp.where(lane < R, l0, pltpu.roll(l1, R, 1)).astype(BF)
+        y = jnp.where(lane < R, rest - l1, pltpu.roll(l0, R, 1)).astype(BF)
         return mm(
-            jnp.concatenate([both, both], axis=1),
-            jnp.concatenate([zh, zh, zl, zl], axis=0),
+            jnp.concatenate([x, x, y], axis=1),
+            jnp.concatenate([z0, z0, z1, z1, z0, z2], axis=0),
         )
 
-    vh, vl = split(start)
-    return lax.fori_loop(0, ITERS, step, image(vh, jnp.concatenate([vh, vl], axis=0)))
-
-
-def masked_factor(halves, start_ref, rank_ref, place_ref, mode, gh_ref, gl_ref):
-    v = subspace(halves, place_ref[0], start_ref[mode], gh_ref, gl_ref)
+    return lax.fori_loop(0, ITERS, step, image(*split3(start)))
+
+
+def masked_factor(halves, start_ref, rank_ref, place_ref, mode, g_ref):
+    v = subspace(halves, place_ref[0], start_ref[mode], g_ref)
     index = lax.broadcasted_iota(jnp.int32, (R, N), 0)
     return jnp.where(index < rank_ref[mode], v, 0.0)
 
@@ -210,11 +218,11 @@
 
 
 def factor_one_kernel(
-    mine_ref, other_ref, start_ref, rank_ref, place_ref, x_hbm, u_ref, a_ref, keep_ref, send_ref, gh_ref, gl_ref, x_ref, sem
+    mine_ref, other_ref, start_ref, rank_ref, place_ref, x_hbm, u_ref, a_ref, keep_ref, send_ref, g_ref, x_ref, sem
 ):
     copy = pltpu.make_async_copy(x_hbm, x_ref, sem)
     copy.start()
-    v = masked_factor((mine_ref, other_ref), start_ref, rank_ref, place_ref, 0, gh_ref, gl_ref)
+    v = masked_factor((mine_ref, other_ref), start_ref, rank_ref, place_ref, 0, g_ref)
     u_ref[...] = v
     vh, vl = split(v)
     vs = jnp.concatenate([vh, vl], axis=0)
@@ -244,8 +252,7 @@
         in_specs=[VMEM, VMEM, VMEM, SMEM, SMEM, HBM],
         out_specs=(VMEM,) * 4,
         scratch_shapes=[
-            pltpu.VMEM((N, N), BF),
-            pltpu.VMEM((N, N), BF),
+            pltpu.VMEM((3, N, N), BF),
             pltpu.VMEM((2, 8, N, N), BF),
             pltpu.SemaphoreType.DMA,
         ],
@@ -255,9 +262,9 @@
 
 
 def factor_two_kernel(
-    mine_ref, other_ref, start_ref, rank_ref, place_ref, a_ref, u_ref, out_ref, gh_ref, gl_ref, y_ref
+    mine_ref, other_ref, start_ref, rank_ref, place_ref, a_ref, u_ref, out_ref, g_ref, y_ref
 ):
-    v = masked_factor((mine_ref, other_ref), start_ref, rank_ref, place_ref, 1, gh_ref, gl_ref)
+    v = masked_factor((mine_ref, other_ref), start_ref, rank_ref, place_ref, 1, g_ref)
     u_ref[...] = v
     vh, vl = split(v)
     vs = jnp.concatenate([vh, vl], axis=0)
@@ -287,7 +294,7 @@
         ),
         in_specs=[VMEM, VMEM, VMEM, SMEM, SMEM, VMEM],
         out_specs=(VMEM, VMEM),
-        scratch_shapes=[pltpu.VMEM((N, N), BF), pltpu.VMEM((N, N), BF), pltpu.VMEM((N, 128), F32)],
+        scratch_shapes=[pltpu.VMEM((3, N, N), BF), pltpu.VMEM((N, 128), F32)],
         compiler_params=pltpu.CompilerParams(vmem_limit_bytes=32 * 2**20),
         name="factor_two",
     )(*halves, starts, ranks, place, a)
@@ -323,9 +330,9 @@
 
 
 def factor_three_kernel(
-    mine_ref, other_ref, start_ref, rank_ref, place_ref, b_ref, u_one_ref, u_two_ref, u_ref, core_ref, gh_ref, gl_ref
+    mine_ref, other_ref, start_ref, rank_ref, place_ref, b_ref, u_one_ref, u_two_ref, u_ref, core_ref, g_ref
 ):
-    v = masked_factor((mine_ref, other_ref), start_ref, rank_ref, place_ref, 2, gh_ref, gl_ref)
+    v = masked_factor((mine_ref, other_ref), start_ref, rank_ref, place_ref, 2, g_ref)
     u_ref[0] = u_one_ref[...]
     u_ref[1] = u_two_ref[...]
     u_ref[2] = v
@@ -348,7 +355,7 @@
         ),
         in_specs=[VMEM, VMEM, VMEM, SMEM, SMEM, VMEM, VMEM, VMEM],
         out_specs=(VMEM, VMEM),
-        scratch_shapes=[pltpu.VMEM((N, N), BF), pltpu.VMEM((N, N), BF)],
+        scratch_shapes=[pltpu.VMEM((3, N, N), BF)],
         compiler_params=pltpu.CompilerParams(vmem_limit_bytes=32 * 2**20),
         name="factor_three",
     )(*halves, starts, ranks, place, b, u_one, u_two)

time: 288 us -> 290 us (level)
  no operation moved by 1% of the time
where the time goes in v6:
time: 290 us; the launch traced here: 289 us
  blocking collectives  227 us (78%)
  Pallas kernels  39.7 us (14%)
  starting transfers between devices  14.1 us (5%)
  waiting for transfers between devices  7.53 us (3%)
    all_to_all x11, blocking collectives, swap(): return lax.all_to_all(x, axes, 0, 0, tiled=True)  227 us
    ppermute x6, starting transfers between devices, other_core(): return lax.ppermute(x, 'core', [(0, 1), (1, 0)])  14.1 us
    pallas_call x1, Pallas kernels, factor_one(): pl.pallas_call(factor_one_kernel, out_shape=(jax.ShapeDtypeStruct((R, N),...  10.2 us
    pallas_call x1, Pallas kernels, factor_two(): pl.pallas_call(factor_two_kernel, out_shape=(jax.ShapeDtypeStruct((R, N),...  8.84 us
    pallas_call x1, Pallas kernels, factor_three(): pl.pallas_call(factor_three_kernel, out_shape=(jax.ShapeDtypeStruct((3, R...  8.63 us
    ppermute x6, waiting for transfers between devices, other_core(): return lax.ppermute(x, 'core', [(0, 1), (1, 0)])  7.53 us
    pallas_call x1, Pallas kernels, gram_one(): pl.pallas_call(gram_one_kernel, grid=(4,), out_shape=(HALF, HALF, pltpu.H...  7.38 us
  transfers between devices with their start and end apart: 6, of which 6 were waited for; matrix products, arithmetic and copies ran while one was open for 0% of the time, Pallas kernels for 0%

profile of v6, /device:TPU:1, one launch (start us, length us, event | category | flops | bytes accessed | tf_op | source)
XLA Modules:
  0.0 289.1 jit_solution(1423063062311702379)
XLA Ops:
  0.6 3.8 %regroup.1 = f32[32,64,8,128]{3,2,1,0:T(8,128)S(1)} custom-call(f32[4,64,64,128]{3,2,1,0:T(8,128)} %x_hbm), custom_call_target="tpu_custom_call" | custom-call | tf_op jit(solution)/shard_map/regroup/pallas_call | solution.py:162
  4.4 103.1 %all_to_all.55 = f32[32,512,128]{2,1,0:T(8,128)S(1)} all-to-all(f32[32,512,128]{2,1,0:T(8,128)S(1)} %bitcast.17), channel_id=1, replica_groups=mesh['y'=4,'core'=2,'gy'=4,'gz'=8] {'y','core','gy'}, dimensions={0} | all-to-all | bytes 16777216 | tf_op jit(solution)/shard_map/all_to_all | solution.py:368
  107.5 7.4 %gram_one.1 = (f32[5,128,128]{2,1,0:T(8,128)S(1)}, f32[5,128,128]{2,1,0:T(8,128)S(1)}, bf16[2,8,512,512]{3,2,1,0:T(8,128)(2,1)}) custom-call(s32[1]{0:T(128)} %bitcast.place_ref, f32[8,4,512,128]{3,2,1,0:T(8,128)S(1)} %bitcast.16), custom_call_target="tpu_custom_call" | custom-call | tf_op jit(solution)/shard_map/gram_one/pallas_call | solution.py:208
  114.9 1.3 collective-permute-start
  116.1 1.3 collective-permute-done
  117.4 12.3 %all_to_all.56 = f32[16,40,128]{2,1,0:T(8,128)S(1)} all-to-all(f32[16,40,128]{2,1,0:T(8,128)S(1)} %bitcast.29), channel_id=1, replica_groups=mesh['y'=4,'core'=2,'gy'=4,'gz'=8] {'y','gy'}, dimensions={0} | all-to-all | bytes 655360 | tf_op jit(solution)/shard_map/all_to_all | solution.py:368
  129.7 16.3 %all_to_all.57 = f32[8,40,128]{2,1,0:T(8,128)S(1)} all-to-all(f32[8,40,128]{2,1,0:T(8,128)S(1)} %broadcast_in_dim.12), channel_id=1, replica_groups=mesh['y'=4,'core'=2,'gy'=4,'gz'=8] {'gz'}, dimensions={0} | all-to-all | bytes 327680 | tf_op jit(solution)/shard_map/all_to_all | solution.py:368
  146.1 10.9 %all_to_all.58 = f32[16,40,128]{2,1,0:T(8,128)S(1)} all-to-all(f32[16,40,128]{2,1,0:T(8,128)S(1)} %broadcast_in_dim.13), channel_id=1, replica_groups=mesh['y'=4,'core'=2,'gy'=4,'gz'=8] {'y','gy'}, dimensions={0} | all-to-all | bytes 655360 | tf_op jit(solution)/shard_map/all_to_all | solution.py:368
  157.0 3.9 %collective-permute-start.1 = (f32[5,128,128]{2,1,0:T(8,128)S(1)}, f32[5,128,128]{2,1,0:T(8,128)S(1)}, u32[]{:S(2)}, u32[]{:S(2)}) collective-permute-start(f32[5,128,128]{2,1,0:T(8,128)S(1)} %bitcast.21), channel_id=1, source_target_pairs={{0,32},{32,0},{1,33},{33,1},{2,34},{34,2},{3,35},{35,3},{4,36},{36... | collective-permute-start | bytes 983048 | tf_op jit(solution)/shard_map/ppermute | solution.py:376
  162.2 10.2 %factor_one.1 = (f32[64,512]{1,0:T(8,128)S(1)}, f32[4,512,128]{2,1,0:T(8,128)S(1)}, f32[5,128,128]{2,1,0:T(8,128)S(1)}, f32[5,128,128]{2,1,0:T(8,128)S(1)}) custom-call(f32[5,128,128]{2,1,0:T(8,128)S(1)} %bitcast.22, f32[5,128,128]{2,1,0:T(8,128)S(1)} %collective-permute-done.1.other_ref, f32[3,64,512]{2,1,0:T(8,128)S(1)} %bitcast.18, s32[3]{0:T(128)S(1)} %copy-done.1, ...), custom_call_target="tpu_custom_call" | custom-call | tf_op jit(solution)/shard_map/factor_one/pallas_call | solution.py:244
  174.2 11.4 %all_to_all.59 = f32[16,40,128]{2,1,0:T(8,128)S(1)} all-to-all(f32[16,40,128]{2,1,0:T(8,128)S(1)} %bitcast.30), channel_id=1, replica_groups=mesh['y'=4,'core'=2,'gy'=4,'gz'=8] {'y','gy'}, dimensions={0} | all-to-all | bytes 655360 | tf_op jit(solution)/shard_map/all_to_all | solution.py:368
  185.7 10.8 %all_to_all.60 = f32[8,40,128]{2,1,0:T(8,128)S(1)} all-to-all(f32[8,40,128]{2,1,0:T(8,128)S(1)} %broadcast_in_dim.14), channel_id=1, replica_groups=mesh['y'=4,'core'=2,'gy'=4,'gz'=8] {'gz'}, dimensions={0} | all-to-all | bytes 327680 | tf_op jit(solution)/shard_map/all_to_all | solution.py:368
  196.5 10.5 %all_to_all.61 = f32[16,40,128]{2,1,0:T(8,128)S(1)} all-to-all(f32[16,40,128]{2,1,0:T(8,128)S(1)} %broadcast_in_dim.15), channel_id=1, replica_groups=mesh['y'=4,'core'=2,'gy'=4,'gz'=8] {'y','gy'}, dimensions={0} | all-to-all | bytes 655360 | tf_op jit(solution)/shard_map/all_to_all | solution.py:368
  207.0 3.9 %collective-permute-start.3 = (f32[5,128,128]{2,1,0:T(8,128)S(1)}, f32[5,128,128]{2,1,0:T(8,128)S(1)}, u32[]{:S(2)}, u32[]{:S(2)}) collective-permute-start(f32[5,128,128]{2,1,0:T(8,128)S(1)} %bitcast.25), channel_id=1, source_target_pairs={{0,32},{32,0},{1,33},{33,1},{2,34},{34,2},{3,35},{35,3},{4,36},{36... | collective-permute-start | bytes 983048 | tf_op jit(solution)/shard_map/ppermute | solution.py:376
  210.9 1.3 collective-permute-done.3.other_ref
  212.2 8.8 %factor_two.1 = (f32[64,512]{1,0:T(8,128)S(1)}, f32[256,128]{1,0:T(8,128)S(1)}) custom-call(f32[5,128,128]{2,1,0:T(8,128)S(1)} %bitcast.26, f32[5,128,128]{2,1,0:T(8,128)S(1)} %collective-permute-done.3.other_ref, f32[3,64,512]{2,1,0:T(8,128)S(1)} %bitcast.19, s32[3]{0:T(128)S(1)} %copy-done.1, s32[1]{0:T(128)} %bitcast.place_ref, ...), custom_call_target="tpu_custom_call" | custom-call | tf_op jit(solution)/shard_map/factor_two/pallas_call | solution.py:289
  221.0 18.3 %all_to_all.62 = f32[256,1,128]{2,1,0:T(1,128)S(1)} all-to-all(f32[256,1,128]{2,1,0:T(1,128)S(1)} %bitcast.28), channel_id=1, replica_groups=mesh['y'=4,'core'=2,'gy'=4,'gz'=8] {'y','core','gy','gz'}, dimensions={0} | all-to-all | bytes 262144 | tf_op jit(solution)/shard_map/all_to_all | solution.py:368
  240.8 1.3 collective-permute-done.4
  242.1 11.7 %all_to_all.63 = f32[16,40,128]{2,1,0:T(8,128)S(1)} all-to-all(f32[16,40,128]{2,1,0:T(8,128)S(1)} %bitcast.31), channel_id=1, replica_groups=mesh['y'=4,'core'=2,'gy'=4,'gz'=8] {'y','gy'}, dimensions={0} | all-to-all | bytes 655360 | tf_op jit(solution)/shard_map/all_to_all | solution.py:368
  253.9 10.8 %all_to_all.64 = f32[8,40,128]{2,1,0:T(8,128)S(1)} all-to-all(f32[8,40,128]{2,1,0:T(8,128)S(1)} %broadcast_in_dim.16), channel_id=1, replica_groups=mesh['y'=4,'core'=2,'gy'=4,'gz'=8] {'gz'}, dimensions={0} | all-to-all | bytes 327680 | tf_op jit(solution)/shard_map/all_to_all | solution.py:368
  264.7 10.6 %all_to_all.65 = f32[16,40,128]{2,1,0:T(8,128)S(1)} all-to-all(f32[16,40,128]{2,1,0:T(8,128)S(1)} %broadcast_in_dim.17), channel_id=1, replica_groups=mesh['y'=4,'core'=2,'gy'=4,'gz'=8] {'y','gy'}, dimensions={0} | all-to-all | bytes 655360 | tf_op jit(solution)/shard_map/all_to_all | solution.py:368
  275.3 3.9 %collective-permute-start.5 = (f32[5,128,128]{2,1,0:T(8,128)S(1)}, f32[5,128,128]{2,1,0:T(8,128)S(1)}, u32[]{:S(2)}, u32[]{:S(2)}) collective-permute-start(f32[5,128,128]{2,1,0:T(8,128)S(1)} %bitcast.23), channel_id=1, source_target_pairs={{0,32},{32,0},{1,33},{33,1},{2,34},{34,2},{3,35},{35,3},{4,36},{36... | collective-permute-start | bytes 983048 | tf_op jit(solution)/shard_map/ppermute | solution.py:376
  279.2 1.3 collective-permute-done.5.other_ref
  280.4 8.6 %factor_three.1 = (f32[3,64,512]{2,1,0:T(8,128)}, f32[4,2,8,64]{3,2,1,0:T(8,128)}) custom-call(f32[5,128,128]{2,1,0:T(8,128)S(1)} %bitcast.24, f32[5,128,128]{2,1,0:T(8,128)S(1)} %collective-permute-done.5.other_ref, f32[3,64,512]{2,1,0:T(8,128)S(1)} %bitcast.20, s32[3]{0:T(128)S(1)} %copy-done.1, s32[1]{0:T(128)} %bitcast.place_ref, ...), custom_call_target="tpu_custom_call" | custom-call | tf_op jit(solution)/shard_map/factor_three/pallas_call | solution.py:350
  (24 shorter events, 4.8 us)
Async XLA Ops:
  107.5 54.7 %copy-start = (f32[3,512,64]{1,2,0:T(8,128)S(1)}, f32[3,512,64]{1,2,0:T(8,128)}, u32[]{:S(2)}) copy-start(f32[3,512,64]{1,2,0:T(8,128)} %param.4) | copy-start | bytes 1179652
  107.5 54.7 %copy-start.1 = (s32[3]{0:T(128)S(1)}, s32[3]{0:T(128)}, u32[]{:S(2)}) copy-start(s32[3]{0:T(128)} %rank_ref.5) | copy-start | bytes 40
  114.9 2.5 collective-permute-start
  157.0 5.2 %collective-permute-start.1 = (f32[5,128,128]{2,1,0:T(8,128)S(1)}, f32[5,128,128]{2,1,0:T(8,128)S(1)}, u32[]{:S(2)}, u32[]{:S(2)}) collective-permute-start(f32[5,128,128]{2,1,0:T(8,128)S(1)} %bitcast.21), channel_id=1, source_target_pairs={{0,32},{32,0},{1,33},{33,1},{2,34},{34,2},{3,35},{35,3},{4,36},{36... | collective-permute-start | bytes 983048 | tf_op jit(solution)/shard_map/ppermute | solution.py:376
  172.4 1.7 collective-permute-start.2
  207.0 5.2 %collective-permute-start.3 = (f32[5,128,128]{2,1,0:T(8,128)S(1)}, f32[5,128,128]{2,1,0:T(8,128)S(1)}, u32[]{:S(2)}, u32[]{:S(2)}) collective-permute-start(f32[5,128,128]{2,1,0:T(8,128)S(1)} %bitcast.25), channel_id=1, source_target_pairs={{0,32},{32,0},{1,33},{33,1},{2,34},{34,2},{3,35},{35,3},{4,36},{36... | collective-permute-start | bytes 983048 | tf_op jit(solution)/shard_map/ppermute | solution.py:376
  240.2 1.9 collective-permute-start.4
  275.3 5.2 %collective-permute-start.5 = (f32[5,128,128]{2,1,0:T(8,128)S(1)}, f32[5,128,128]{2,1,0:T(8,128)S(1)}, u32[]{:S(2)}, u32[]{:S(2)}) collective-permute-start(f32[5,128,128]{2,1,0:T(8,128)S(1)} %bitcast.23), channel_id=1, source_target_pairs={{0,32},{32,0},{1,33},{33,1},{2,34},{34,2},{3,35},{35,3},{4,36},{36... | collective-permute-start | bytes 983048 | tf_op jit(solution)/shard_map/ppermute | solution.py:376

commit v7 on v6

--- a/solution.py
+++ b/solution.py
@@ -41,6 +41,8 @@
         def _():
             for n, (a, b) in enumerate(PAIRS):
                 out_ref = keep_ref if n // 5 == here else send_ref
+                if out_ref is None:
+                    continue
                 if a < 2:
                     out_ref[n % 5] = low[a * 128 : a * 128 + 128, b * 128 : b * 128 + 128]
                 else:
@@ -300,33 +302,33 @@
     )(*halves, starts, ranks, place, a)
 
 
-def gram_three_kernel(place_ref, y_ref, keep_ref, send_ref, b_ref):
+def gram_three_kernel(place_ref, y_ref, other_ref, keep_ref, b_ref):
     group = lax.broadcasted_iota(jnp.int32, (8, 128), 1) // 16
     for pg in range(8):
         for p in range(8):
             rows = jnp.zeros((8, 128), F32)
-            for s in range(4):
-                at = (8 * s + pg) * 8
-                tile = y_ref[at : at + 8, :]
-                if s != p:
-                    tile = pltpu.roll(tile, (16 * (s - p)) % 128, 1)
-                rows = jnp.where(group == s, tile, rows)
+            for g in range(8):
+                at = (8 * (g % 4) + pg) * 8
+                tile = (y_ref if g < 4 else other_ref)[at : at + 8, :]
+                if g != p:
+                    tile = pltpu.roll(tile, (16 * (g - p)) % 128, 1)
+                rows = jnp.where(group == g, tile, rows)
             b_ref[pl.ds(8 * pg + p, 8, stride=R), :] = rows
     bh, bl = split(b_ref[...])
     low = mm(bh[:256], bh, NT) + mm(bh[:256], bl, NT) + mm(bl[:256], bh, NT)
     high = mm(bh[256:], bh[256:], NT) + mm(bh[256:], bl[256:], NT) + mm(bl[256:], bh[256:], NT)
-    put_blocks(keep_ref, send_ref, place_ref[0], low * 2.0**-20, high * 2.0**-20)
-
-
-def gram_three(place, y):
+    put_blocks(keep_ref, None, place_ref[0], low * 2.0**-20, high * 2.0**-20)
+
+
+def gram_three(place, y, other):
     return pl.pallas_call(
         gram_three_kernel,
-        out_shape=(HALF, HALF, jax.ShapeDtypeStruct((N, 128), F32)),
-        in_specs=[SMEM, VMEM],
-        out_specs=(VMEM, VMEM, VMEM),
+        out_shape=(HALF, jax.ShapeDtypeStruct((N, 128), F32)),
+        in_specs=[SMEM, VMEM, VMEM],
+        out_specs=(VMEM, VMEM),
         compiler_params=pltpu.CompilerParams(vmem_limit_bytes=32 * 2**20),
         name="gram_three",
-    )(place, y)
+    )(place, y, other)
 
 
 def factor_three_kernel(
@@ -376,8 +378,7 @@
     return lax.ppermute(x, "core", [(0, 1), (1, 0)])
 
 
-def total(keep, send):
-    g = keep + other_core(send)
+def total(g):
     g = jnp.sum(swap(g.reshape(16, 40, 128), PLANE), axis=0)
     g = jnp.sum(spread(g, "gz", 8), axis=0)
     g = spread(g, PLANE, 16).reshape(5, 128, 128)
@@ -391,11 +392,11 @@
     x = regroup(tensor).reshape(32, N, 128)
     x = swap(x, ("y", "core", "gy")).reshape(8, 4, N, 128)
     keep, send, x2 = gram_one(place, x)
-    u_one, a, keep, send = factor_one(total(keep, send), starts_t, trunc_ranks, place, x2)
-    u_two, y = factor_two(total(keep, send), starts_t, trunc_ranks, place, a)
+    u_one, a, keep, send = factor_one(total(keep + other_core(send)), starts_t, trunc_ranks, place, x2)
+    u_two, y = factor_two(total(keep + other_core(send)), starts_t, trunc_ranks, place, a)
     y = swap(y.reshape(256, 1, 128), ("y", "core", "gy", "gz")).reshape(256, 128)
-    keep, send, b = gram_three(place, y)
-    factors, core_out = factor_three(total(keep, send), starts_t, trunc_ranks, place, b, u_one, u_two)
+    g, b = gram_three(place, y, other_core(y))
+    factors, core_out = factor_three(total(g), starts_t, trunc_ranks, place, b, u_one, u_two)
     return (jnp.swapaxes(core_out, 2, 3), jnp.swapaxes(factors, 1, 2))
 
 

time: 290 us -> 289 us (level)
  no operation moved by 1% of the time
where the time goes in v7:
time: 289 us
  blocking collectives  227 us (79%)
  Pallas kernels  39.9 us (14%)
  starting transfers between devices  14 us (5%)
  waiting for transfers between devices  7.27 us (3%)
    all_to_all x11, blocking collectives, swap(): return lax.all_to_all(x, axes, 0, 0, tiled=True)  227 us
    ppermute x6, starting transfers between devices, other_core(): return lax.ppermute(x, 'core', [(0, 1), (1, 0)])  14 us
    pallas_call x1, Pallas kernels, factor_one(): pl.pallas_call(factor_one_kernel, out_shape=(jax.ShapeDtypeStruct((R, N),...  10.2 us
    pallas_call x1, Pallas kernels, factor_two(): pl.pallas_call(factor_two_kernel, out_shape=(jax.ShapeDtypeStruct((R, N),...  8.84 us
    pallas_call x1, Pallas kernels, factor_three(): pl.pallas_call(factor_three_kernel, out_shape=(jax.ShapeDtypeStruct((3, R...  8.64 us
    pallas_call x1, Pallas kernels, gram_one(): pl.pallas_call(gram_one_kernel, grid=(4,), out_shape=(HALF, HALF, pltpu.H...  7.38 us
    ppermute x6, waiting for transfers between devices, other_core(): return lax.ppermute(x, 'core', [(0, 1), (1, 0)])  7.27 us
  transfers between devices with their start and end apart: 6, of which 6 were waited for; matrix products, arithmetic and copies ran while one was open for 0% of the time, Pallas kernels for 0%

profile of v7, /device:TPU:1, one launch (start us, length us, event | category | flops | bytes accessed | tf_op | source)
XLA Modules:
  0.0 288.9 jit_solution(1006268600819191709)
XLA Ops:
  0.6 3.8 %regroup.1 = f32[32,64,8,128]{3,2,1,0:T(8,128)S(1)} custom-call(f32[4,64,64,128]{3,2,1,0:T(8,128)} %x_hbm), custom_call_target="tpu_custom_call" | custom-call | tf_op jit(solution)/shard_map/regroup/pallas_call | solution.py:164
  4.4 103.1 %all_to_all.55 = f32[32,512,128]{2,1,0:T(8,128)S(1)} all-to-all(f32[32,512,128]{2,1,0:T(8,128)S(1)} %bitcast.17), channel_id=1, replica_groups=mesh['y'=4,'core'=2,'gy'=4,'gz'=8] {'y','core','gy'}, dimensions={0} | all-to-all | bytes 16777216 | tf_op jit(solution)/shard_map/all_to_all | solution.py:370
  107.5 7.4 %gram_one.1 = (f32[5,128,128]{2,1,0:T(8,128)S(1)}, f32[5,128,128]{2,1,0:T(8,128)S(1)}, bf16[2,8,512,512]{3,2,1,0:T(8,128)(2,1)}) custom-call(s32[1]{0:T(128)} %bitcast.place_ref, f32[8,4,512,128]{3,2,1,0:T(8,128)S(1)} %bitcast.16), custom_call_target="tpu_custom_call" | custom-call | tf_op jit(solution)/shard_map/gram_one/pallas_call | solution.py:210
  114.9 1.3 collective-permute-start
  116.1 1.3 collective-permute-done
  117.4 12.3 %all_to_all.56 = f32[16,40,128]{2,1,0:T(8,128)S(1)} all-to-all(f32[16,40,128]{2,1,0:T(8,128)S(1)} %bitcast.31), channel_id=1, replica_groups=mesh['y'=4,'core'=2,'gy'=4,'gz'=8] {'y','gy'}, dimensions={0} | all-to-all | bytes 655360 | tf_op jit(solution)/shard_map/all_to_all | solution.py:370
  129.7 16.3 %all_to_all.57 = f32[8,40,128]{2,1,0:T(8,128)S(1)} all-to-all(f32[8,40,128]{2,1,0:T(8,128)S(1)} %broadcast_in_dim.12), channel_id=1, replica_groups=mesh['y'=4,'core'=2,'gy'=4,'gz'=8] {'gz'}, dimensions={0} | all-to-all | bytes 327680 | tf_op jit(solution)/shard_map/all_to_all | solution.py:370
  146.1 10.9 %all_to_all.58 = f32[16,40,128]{2,1,0:T(8,128)S(1)} all-to-all(f32[16,40,128]{2,1,0:T(8,128)S(1)} %broadcast_in_dim.13), channel_id=1, replica_groups=mesh['y'=4,'core'=2,'gy'=4,'gz'=8] {'y','gy'}, dimensions={0} | all-to-all | bytes 655360 | tf_op jit(solution)/shard_map/all_to_all | solution.py:370
  157.0 3.9 %collective-permute-start.1 = (f32[5,128,128]{2,1,0:T(8,128)S(1)}, f32[5,128,128]{2,1,0:T(8,128)S(1)}, u32[]{:S(2)}, u32[]{:S(2)}) collective-permute-start(f32[5,128,128]{2,1,0:T(8,128)S(1)} %bitcast.21), channel_id=1, source_target_pairs={{0,32},{32,0},{1,33},{33,1},{2,34},{34,2},{3,35},{35,3},{4,36},{36... | collective-permute-start | bytes 983048 | tf_op jit(solution)/shard_map/ppermute | solution.py:378
  160.9 1.3 collective-permute-done.1.other_ref
  162.2 10.2 %factor_one.1 = (f32[64,512]{1,0:T(8,128)S(1)}, f32[4,512,128]{2,1,0:T(8,128)S(1)}, f32[5,128,128]{2,1,0:T(8,128)S(1)}, f32[5,128,128]{2,1,0:T(8,128)S(1)}) custom-call(f32[5,128,128]{2,1,0:T(8,128)S(1)} %bitcast.22, f32[5,128,128]{2,1,0:T(8,128)S(1)} %collective-permute-done.1.other_ref, f32[3,64,512]{2,1,0:T(8,128)S(1)} %bitcast.18, s32[3]{0:T(128)S(1)} %copy-done.1, ...), custom_call_target="tpu_custom_call" | custom-call | tf_op jit(solution)/shard_map/factor_one/pallas_call | solution.py:246
  172.9 1.3 collective-permute-done.2
  174.2 11.4 %all_to_all.59 = f32[16,40,128]{2,1,0:T(8,128)S(1)} all-to-all(f32[16,40,128]{2,1,0:T(8,128)S(1)} %bitcast.32), channel_id=1, replica_groups=mesh['y'=4,'core'=2,'gy'=4,'gz'=8] {'y','gy'}, dimensions={0} | all-to-all | bytes 655360 | tf_op jit(solution)/shard_map/all_to_all | solution.py:370
  185.7 10.8 %all_to_all.60 = f32[8,40,128]{2,1,0:T(8,128)S(1)} all-to-all(f32[8,40,128]{2,1,0:T(8,128)S(1)} %broadcast_in_dim.14), channel_id=1, replica_groups=mesh['y'=4,'core'=2,'gy'=4,'gz'=8] {'gz'}, dimensions={0} | all-to-all | bytes 327680 | tf_op jit(solution)/shard_map/all_to_all | solution.py:370
  196.5 10.5 %all_to_all.61 = f32[16,40,128]{2,1,0:T(8,128)S(1)} all-to-all(f32[16,40,128]{2,1,0:T(8,128)S(1)} %broadcast_in_dim.15), channel_id=1, replica_groups=mesh['y'=4,'core'=2,'gy'=4,'gz'=8] {'y','gy'}, dimensions={0} | all-to-all | bytes 655360 | tf_op jit(solution)/shard_map/all_to_all | solution.py:370
  207.0 3.9 %collective-permute-start.3 = (f32[5,128,128]{2,1,0:T(8,128)S(1)}, f32[5,128,128]{2,1,0:T(8,128)S(1)}, u32[]{:S(2)}, u32[]{:S(2)}) collective-permute-start(f32[5,128,128]{2,1,0:T(8,128)S(1)} %bitcast.25), channel_id=1, source_target_pairs={{0,32},{32,0},{1,33},{33,1},{2,34},{34,2},{3,35},{35,3},{4,36},{36... | collective-permute-start | bytes 983048 | tf_op jit(solution)/shard_map/ppermute | solution.py:378
  210.9 1.3 collective-permute-done.3.other_ref
  212.2 8.8 %factor_two.1 = (f32[64,512]{1,0:T(8,128)S(1)}, f32[256,128]{1,0:T(8,128)S(1)}) custom-call(f32[5,128,128]{2,1,0:T(8,128)S(1)} %bitcast.26, f32[5,128,128]{2,1,0:T(8,128)S(1)} %collective-permute-done.3.other_ref, f32[3,64,512]{2,1,0:T(8,128)S(1)} %bitcast.19, s32[3]{0:T(128)S(1)} %copy-done.1, s32[1]{0:T(128)} %bitcast.place_ref, ...), custom_call_target="tpu_custom_call" | custom-call | tf_op jit(solution)/shard_map/factor_two/pallas_call | solution.py:291
  221.0 18.3 %all_to_all.62 = f32[256,1,128]{2,1,0:T(1,128)S(1)} all-to-all(f32[256,1,128]{2,1,0:T(1,128)S(1)} %bitcast.30), channel_id=1, replica_groups=mesh['y'=4,'core'=2,'gy'=4,'gz'=8] {'y','core','gy','gz'}, dimensions={0} | all-to-all | bytes 262144 | tf_op jit(solution)/shard_map/all_to_all | solution.py:370
  241.9 11.8 %all_to_all.63 = f32[16,40,128]{2,1,0:T(8,128)S(1)} all-to-all(f32[16,40,128]{2,1,0:T(8,128)S(1)} %bitcast.29), channel_id=1, replica_groups=mesh['y'=4,'core'=2,'gy'=4,'gz'=8] {'y','gy'}, dimensions={0} | all-to-all | bytes 655360 | tf_op jit(solution)/shard_map/all_to_all | solution.py:370
  253.7 10.8 %all_to_all.64 = f32[8,40,128]{2,1,0:T(8,128)S(1)} all-to-all(f32[8,40,128]{2,1,0:T(8,128)S(1)} %broadcast_in_dim.16), channel_id=1, replica_groups=mesh['y'=4,'core'=2,'gy'=4,'gz'=8] {'gz'}, dimensions={0} | all-to-all | bytes 327680 | tf_op jit(solution)/shard_map/all_to_all | solution.py:370
  264.6 10.6 %all_to_all.65 = f32[16,40,128]{2,1,0:T(8,128)S(1)} all-to-all(f32[16,40,128]{2,1,0:T(8,128)S(1)} %broadcast_in_dim.17), channel_id=1, replica_groups=mesh['y'=4,'core'=2,'gy'=4,'gz'=8] {'y','gy'}, dimensions={0} | all-to-all | bytes 655360 | tf_op jit(solution)/shard_map/all_to_all | solution.py:370
  275.1 3.9 %collective-permute-start.5 = (f32[5,128,128]{2,1,0:T(8,128)S(1)}, f32[5,128,128]{2,1,0:T(8,128)S(1)}, u32[]{:S(2)}, u32[]{:S(2)}) collective-permute-start(f32[5,128,128]{2,1,0:T(8,128)S(1)} %bitcast.23), channel_id=1, source_target_pairs={{0,32},{32,0},{1,33},{33,1},{2,34},{34,2},{3,35},{35,3},{4,36},{36... | collective-permute-start | bytes 983048 | tf_op jit(solution)/shard_map/ppermute | solution.py:378
  280.3 8.6 %factor_three.1 = (f32[3,64,512]{2,1,0:T(8,128)}, f32[4,2,8,64]{3,2,1,0:T(8,128)}) custom-call(f32[5,128,128]{2,1,0:T(8,128)S(1)} %bitcast.24, f32[5,128,128]{2,1,0:T(8,128)S(1)} %collective-permute-done.5.other_ref, f32[3,64,512]{2,1,0:T(8,128)S(1)} %bitcast.20, s32[3]{0:T(128)S(1)} %copy-done.1, s32[1]{0:T(128)} %bitcast.place_ref, ...), custom_call_target="tpu_custom_call" | custom-call | tf_op jit(solution)/shard_map/factor_three/pallas_call | solution.py:352
  (23 shorter events, 4.7 us)
Async XLA Ops:
  107.5 54.7 %copy-start = (f32[3,512,64]{1,2,0:T(8,128)S(1)}, f32[3,512,64]{1,2,0:T(8,128)}, u32[]{:S(2)}) copy-start(f32[3,512,64]{1,2,0:T(8,128)} %param.4) | copy-start | bytes 1179652
  107.5 54.7 %copy-start.1 = (s32[3]{0:T(128)S(1)}, s32[3]{0:T(128)}, u32[]{:S(2)}) copy-start(s32[3]{0:T(128)} %rank_ref.5) | copy-start | bytes 40
  114.9 2.5 collective-permute-start
  157.0 5.2 %collective-permute-start.1 = (f32[5,128,128]{2,1,0:T(8,128)S(1)}, f32[5,128,128]{2,1,0:T(8,128)S(1)}, u32[]{:S(2)}, u32[]{:S(2)}) collective-permute-start(f32[5,128,128]{2,1,0:T(8,128)S(1)} %bitcast.21), channel_id=1, source_target_pairs={{0,32},{32,0},{1,33},{33,1},{2,34},{34,2},{3,35},{35,3},{4,36},{36... | collective-permute-start | bytes 983048 | tf_op jit(solution)/shard_map/ppermute | solution.py:378
  172.4 1.7 collective-permute-start.2
  207.0 5.2 %collective-permute-start.3 = (f32[5,128,128]{2,1,0:T(8,128)S(1)}, f32[5,128,128]{2,1,0:T(8,128)S(1)}, u32[]{:S(2)}, u32[]{:S(2)}) collective-permute-start(f32[5,128,128]{2,1,0:T(8,128)S(1)} %bitcast.25), channel_id=1, source_target_pairs={{0,32},{32,0},{1,33},{33,1},{2,34},{34,2},{3,35},{35,3},{4,36},{36... | collective-permute-start | bytes 983048 | tf_op jit(solution)/shard_map/ppermute | solution.py:378
  239.3 1.5 collective-permute-start.4
  275.1 5.2 %collective-permute-start.5 = (f32[5,128,128]{2,1,0:T(8,128)S(1)}, f32[5,128,128]{2,1,0:T(8,128)S(1)}, u32[]{:S(2)}, u32[]{:S(2)}) collective-permute-start(f32[5,128,128]{2,1,0:T(8,128)S(1)} %bitcast.23), channel_id=1, source_target_pairs={{0,32},{32,0},{1,33},{33,1},{2,34},{34,2},{3,35},{35,3},{4,36},{36... | collective-permute-start | bytes 983048 | tf_op jit(solution)/shard_map/ppermute | solution.py:378
